TPU v7x, 32 devices: a whole 2x2x4 slice. The times are simulated.
32 devices in a mesh: dp: 8 (over y, x, core), mp: 4 (over z).
Axes of the slice: x: 2, y: 2, z: 4, core: 2. Of those that a mesh axis runs over, the one named last changes fastest.
Arguments:
- tokens: bfloat16 [16384, 768], P(('dp', 'mp')), may hold values from -6 to 6
- segments: int32 [8, 2048], P('dp'), may hold values from -1 to 2048, as said below
- out_grad: bfloat16 [16384, 768], P(('dp', 'mp')), may hold values from -6 to 6
- align_grad: bfloat16 [16384, 1024], P(('dp', 'mp')), may hold values from -6 to 6
- first_gain: bfloat16 [768], P(('dp', 'mp')), may hold values from 0.5 to 1.5
- first_shift: bfloat16 [768], P(('dp', 'mp')), may hold values from -1.75 to 1.75
- joint_weight: bfloat16 [768, 2304], P(('dp', 'mp')), may hold values from -0.21875 to 0.21875
- query_bias: bfloat16 [768], P(('dp', 'mp')), may hold values from -3 to 3
- value_bias: bfloat16 [768], P(('dp', 'mp')), may hold values from -3 to 3
- output_weight: bfloat16 [768, 768], P(('dp', 'mp')), may hold values from -0.875 to 0.875
- output_bias: bfloat16 [768], P(('dp', 'mp')), may hold values from -1.75 to 1.75
- second_gain: bfloat16 [768], P(('dp', 'mp')), may hold values from 0.5 to 1.5
- second_shift: bfloat16 [768], P(('dp', 'mp')), may hold values from -1.75 to 1.75
- expand_bias: bfloat16 [3072], P(('dp', 'mp')), may hold values from -3 to 3
- reduce_bias: bfloat16 [768], P(('dp', 'mp')), may hold values from -1.75 to 1.75
- head_gain: bfloat16 [768], P(('dp', 'mp')), may hold values from 0.5 to 1.5
- head_shift: bfloat16 [768], P(('dp', 'mp')), may hold values from -1.75 to 1.75
- align_weight: bfloat16 [768, 1024], P(('dp', 'mp')), may hold values from -0.21875 to 0.21875
- align_bias: bfloat16 [1024], P(('dp', 'mp')), may hold values from -3 to 3
- expand_weight: bfloat16 [768, 3072], P('dp', 'mp'), may hold values from -0.21875 to 0.21875
- reduce_weight: bfloat16 [3072, 768], P('mp', 'dp'), may hold values from -0.109375 to 0.109375
Outputs:
- block_out: bfloat16 [16384, 768], P(('dp', 'mp'))
- align_out: bfloat16 [16384, 1024], P(('dp', 'mp'))
- tokens_grad: float32 [16384, 768], P(('dp', 'mp'))
- first_gain_grad: float32 [768], P(('dp', 'mp'))
- first_shift_grad: float32 [768], P(('dp', 'mp'))
- joint_weight_grad: float32 [768, 2304], P(('dp', 'mp'))
- query_bias_grad: float32 [768], P(('dp', 'mp'))
- value_bias_grad: float32 [768], P(('dp', 'mp'))
- output_weight_grad: float32 [768, 768], P(('dp', 'mp'))
- output_bias_grad: float32 [768], P(('dp', 'mp'))
- second_gain_grad: float32 [768], P(('dp', 'mp'))
- second_shift_grad: float32 [768], P(('dp', 'mp'))
- expand_bias_grad: float32 [3072], P(('dp', 'mp'))
- reduce_bias_grad: float32 [768], P(('dp', 'mp'))
- head_gain_grad: float32 [768], P(('dp', 'mp'))
- head_shift_grad: float32 [768], P(('dp', 'mp'))
- align_weight_grad: float32 [768, 1024], P(('dp', 'mp'))
- align_bias_grad: float32 [1024], P(('dp', 'mp'))
- expand_weight_grad: float32 [768, 3072], P('dp', 'mp')
- reduce_weight_grad: float32 [3072, 768], P('mp', 'dp')
Inputs may be any that keep to these rules, and one draw needn't show every extreme that they name: `segments`: segment numbers never fall along a row; padding slots carry -1 and stand at the end of a row, every row having some; the last segment before the padding is numbered 2048 in every row; in every row one segment starts within the first 256 slots and ends after slot 1536.
All inputs are finite; a program needn't handle non-finite values.
Results may differ from a plain program's by a relative error of at most 0.014.
Values may be sent and summed in bfloat16 or wider, within the bound.
A program may use at most 192 MiB of HBM per device.

v0:
```python
import functools

import jax
import jax.numpy as jnp
from jax import lax
from jax.experimental import pallas as pl
from jax.experimental.pallas import tpu as pltpu
from jax.sharding import PartitionSpec as P

H = 12
HD = 64
EPSILON = 1e-06
NEG_FILL = -1000000000.0
MESH = pl.DeviceIdType.MESH
VMEM_LIMIT = 56 << 20


def layer_norm(values, gain, shift):
    centre = values - jnp.mean(values, axis=-1, keepdims=True)
    spread = jnp.mean(centre * centre, axis=-1, keepdims=True)
    return centre * lax.rsqrt(spread + EPSILON) * gain + shift


def nn(left, right):
    return lax.dot_general(
        left, right, (((1,), (0,)), ((), ())), preferred_element_type=jnp.float32
    )


def nt(left, right):
    return lax.dot_general(
        left, right, (((1,), (1,)), ((), ())), preferred_element_type=jnp.float32
    )


ANY = pl.BlockSpec(memory_space=pl.ANY)
VM = pl.BlockSpec(memory_space=pltpu.VMEM)


def peer_flip(index, bit):
    return index + bit * (1 - 2 * (index // bit % 2))


def mask_flip(index, mask):
    bit = 1
    while bit <= mask:
        if mask & bit:
            index = peer_flip(index, bit)
        bit *= 2
    return index


def plane_masks(order, step):
    masks = [0]
    for bit in order[:step]:
        masks += [m ^ bit for m in masks]
    return masks


class Spread:
    def __init__(self, slot, own, full, wide, nd, nz, dp, z, sems):
        self.slot, self.own, self.full, self.wide = slot, own, full, wide
        self.nd, self.nz, self.dp, self.z = nd, nz, dp, z
        self.keep_sem, self.right_sem, self.left_sem, self.line_sem, self.send_sem, self.recv_sem = sems
        self.bits = [1 << b for b in range(1, nd.bit_length() - 1)]
        self.cut = nz // 2

    def order(self, half):
        return self.bits if half == 0 else self.bits[::-1]

    def chunk(self, j):
        if self.wide:
            cols = self.own.shape[1]
            return self.full.at[self.dp, :, pl.ds(pl.multiple_of(j * cols, 128), cols)]
        return self.full.at[self.dp, j]

    def block(self, half, mask):
        d = mask_flip(self.dp, mask)
        lo, hi = (0, self.cut) if half == 0 else (self.cut, self.nz)
        if self.wide:
            cols = self.own.shape[1]
            return self.full.at[d, :, pl.ds(lo * cols, (hi - lo) * cols)]
        return self.full.at[d, pl.ds(lo, hi - lo)]

    def keep(self):
        return pltpu.make_async_copy(self.own, self.chunk(self.z), self.keep_sem.at[self.slot])

    def _right(self, step):
        j = jnp.maximum(self.z - step, 0)
        return pltpu.make_async_remote_copy(
            src_ref=self.own if step == 0 else self.chunk(j),
            dst_ref=self.chunk(j),
            send_sem=self.right_sem.at[self.slot, step],
            recv_sem=self.line_sem.at[self.slot, j],
            device_id=(self.dp, jnp.minimum(self.z + 1, self.nz - 1)),
            device_id_type=MESH,
        )

    def _left(self, step):
        j = jnp.minimum(self.z + step, self.nz - 1)
        return pltpu.make_async_remote_copy(
            src_ref=self.own if step == 0 else self.chunk(j),
            dst_ref=self.chunk(j),
            send_sem=self.left_sem.at[self.slot, step],
            recv_sem=self.line_sem.at[self.slot, j],
            device_id=(self.dp, jnp.maximum(self.z - 1, 0)),
            device_id_type=MESH,
        )

    def line_start(self, step):
        if step >= self.nz - 1:
            return

        @pl.when((self.z < self.nz - 1) & (self.z - step >= 0))
        def _():
            self._right(step).start()

        @pl.when((self.z > 0) & (self.z + step <= self.nz - 1))
        def _():
            self._left(step).start()

    def line_wait(self, step):
        @pl.when(self.z - step >= 0)
        def _():
            self._right(step).wait_recv()

        @pl.when(self.z + step <= self.nz - 1)
        def _():
            self._left(step).wait_recv()

    def _plane(self, half, mask, bit):
        return pltpu.make_async_remote_copy(
            src_ref=self.block(half, mask),
            dst_ref=self.block(half, mask),
            send_sem=self.send_sem.at[self.slot, half, mask ^ bit],
            recv_sem=self.recv_sem.at[self.slot, half, mask ^ bit],
            device_id=(peer_flip(self.dp, bit), self.z),
            device_id_type=MESH,
        )

    def _arrival(self, half, mask, bit):
        return pltpu.make_async_remote_copy(
            src_ref=self.block(half, mask),
            dst_ref=self.block(half, mask),
            send_sem=self.send_sem.at[self.slot, half, mask],
            recv_sem=self.recv_sem.at[self.slot, half, mask],
            device_id=(peer_flip(self.dp, bit), self.z),
            device_id_type=MESH,
        )

    def plane_start(self, step):
        if step >= len(self.bits):
            return
        for half in range(2):
            order = self.order(half)
            for mask in plane_masks(order, step):
                self._plane(half, mask, order[step]).start()

    def plane_wait(self, step):
        for half in range(2):
            order = self.order(half)
            for mask in plane_masks(order, step):
                self._arrival(half, mask ^ order[step], order[step]).wait_recv()

    def _new_masks(self, half, step):
        order = self.order(half)
        return [0] if step < 0 else [m ^ order[step] for m in plane_masks(order, step)]

    def core_start(self, step):
        for half in range(2):
            for mask in self._new_masks(half, step):
                self._plane(half, mask, 1).start()

    def core_wait(self):
        for half in range(2):
            for mask in plane_masks(self.bits, len(self.bits)):
                self._arrival(half, mask ^ 1, 1).wait_recv()

    def sends_wait(self):
        for step in range(self.nz - 1):

            @pl.when((self.z < self.nz - 1) & (self.z - step >= 0))
            def _():
                self._right(step).wait_send()

            @pl.when((self.z > 0) & (self.z + step <= self.nz - 1))
            def _():
                self._left(step).wait_send()

        for half in range(2):
            order = self.order(half)
            for step in range(len(self.bits)):
                for mask in plane_masks(order, step):
                    self._plane(half, mask, order[step]).wait_send()
            for mask in plane_masks(order, len(self.bits)):
                self._plane(half, mask, 1).wait_send()


def greet(nd, nz, dp, z, line=True, plane=True):
    barrier = pltpu.get_barrier_semaphore()
    count = 0
    if line:
        for off in range(1, nz):
            pl.semaphore_signal(
                barrier, inc=1, device_id=(dp, lax.rem(z + off, nz)), device_id_type=MESH
            )
            count += 1
    if plane:
        bit = 1
        while bit < nd:
            pl.semaphore_signal(
                barrier, inc=1, device_id=(peer_flip(dp, bit), z), device_id_type=MESH
            )
            count += 1
            bit *= 2
    pl.semaphore_wait(barrier, count)


def lane_copies(seg_row):
    return jnp.broadcast_to(seg_row[...], (128, seg_row.shape[1])).T


def forward_kernel(
    nd,
    nz,
    nh,
    x_own,
    vec_own,
    joint_own,
    wo_own,
    wa_own,
    w1_own,
    w2_own,
    seg_row,
    vec_rows,
    joint,
    wo,
    wa,
    w1,
    w2,
    normed_out,
    qkv_out,
    att_out,
    lse,
    att_land,
    x_land,
    vec,
    window,
    vec_cols,
    weights,
    weights_t,
    wide,
    normed,
    qkv,
    att,
    keys,
    bias,
    seg_lanes,
    tops,
    totals,
    att_send,
    keep_sem,
    right_sem,
    left_sem,
    line_sem,
    send_sem,
    recv_sem,
    x_sem,
    x_right,
    x_left,
    x_recv,
    win_sem,
    att_send_sem,
    att_recv_sem,
    out_sem,
):
    dp, z = lax.axis_index("dp"), lax.axis_index("mp")
    rows, width = x_own.shape
    seq = rows * nz
    own_cols = nh * HD
    win_cols = window.shape[-1] // 3
    win = z * own_cols // 128 * 128
    shift = pl.multiple_of(z * own_cols - win, HD)
    win = pl.multiple_of(win, 128)
    f32, b16 = jnp.float32, jnp.bfloat16
    sems = (keep_sem, right_sem, left_sem, line_sem, send_sem, recv_sem)
    specs = [
        (vec_own, vec, False),
        (joint_own, joint, False),
        (wo_own, wo, False),
        (w1_own, w1, True),
        (wa_own, wa, False),
        (w2_own, w2, True),
    ]
    spreads = [Spread(i, *spec, nd, nz, dp, z, sems) for i, spec in enumerate(specs)]
    first, second, third = spreads[:2], spreads[2:4], spreads[4:]
    steps = len(spreads[0].bits)

    def line_step(group, step):
        for s in group:
            s.line_wait(step)
            s.line_start(step)

    def plane_open(group):
        for s in group:
            s.keep().wait()
            s.plane_start(0)
            s.core_start(-1)

    def plane_step(group, step):
        for s in group:
            s.plane_wait(step)
            s.plane_start(step + 1)
            s.core_start(step)

    def x_to_right(step):
        j = jnp.maximum(z - step, 0)
        return pltpu.make_async_remote_copy(
            src_ref=x_land.at[j],
            dst_ref=x_land.at[j],
            send_sem=x_right.at[step],
            recv_sem=x_recv.at[j],
            device_id=(dp, jnp.minimum(z + 1, nz - 1)),
            device_id_type=MESH,
        )

    def x_to_left(step):
        j = jnp.minimum(z + step, nz - 1)
        return pltpu.make_async_remote_copy(
            src_ref=x_land.at[j],
            dst_ref=x_land.at[j],
            send_sem=x_left.at[step],
            recv_sem=x_recv.at[j],
            device_id=(dp, jnp.maximum(z - 1, 0)),
            device_id_type=MESH,
        )

    def x_start(step):
        @pl.when((z < nz - 1) & (z - step >= 0))
        def _():
            x_to_right(step).start()

        @pl.when((z > 0) & (z + step <= nz - 1))
        def _():
            x_to_left(step).start()

    greet(nd, nz, dp, z)
    for s in spreads:
        s.keep().start()
    x_keep = pltpu.make_async_copy(x_own, x_land.at[z], x_sem)
    x_keep.start()
    for s in first:
        s.line_start(0)
    for step in range(1, nz - 1):
        line_step(first, step)
    for s in second:
        s.line_start(0)
    seg_lanes[...] = lane_copies(seg_row)
    line_step(first, nz - 1)
    plane_open(first)
    line_step(second, 1)
    plane_step(first, 0)
    for step in range(2, nz - 1):
        line_step(second, step)
    for s in third:
        s.line_start(0)
    line_step(second, nz - 1)
    plane_open(second)
    line_step(third, 1)
    for t in range(1, steps):
        plane_step(first, t)
    for step in range(2, nz - 1):
        line_step(third, step)
    x_keep.wait()
    x_start(0)
    line_step(third, nz - 1)
    plane_open(third)
    plane_step(second, 0)
    for s in first:
        s.core_wait()

    loads = []
    for p in range(3):
        load = pltpu.make_async_copy(
            joint.at[:, :, :, pl.ds(pl.multiple_of(p * width + win, 128), win_cols)],
            window.at[:, :, :, pl.ds(p * win_cols, win_cols)],
            win_sem.at[p],
        )
        load.start()
        loads.append(load)
    own = vec.shape[2]
    for d in range(nd):
        for j in range(nz):
            at = (d * nz + j) * own
            vec_cols[at : at + own, :] = vec[d, j].astype(f32)
    vec_t = vec_cols[...].T
    vec_rows[...] = vec_t[: vec_rows.shape[0]]
    for load in loads:
        load.wait()
    for d in range(nd):
        for j in range(nz):
            at = (d * nz + j) * own
            weights[at : at + own, :] = window[d, j].astype(f32)
    for p in range(3):
        cols = slice(p * win_cols, (p + 1) * win_cols)
        weights_t[cols, :] = weights[:, cols].T.astype(b16)
    gain, offset = vec_rows[0:1, :], vec_rows[1:2, :]
    bias_q = vec_cols[pl.ds(win, win_cols), 2:3]
    bias_v = vec_cols[pl.ds(win, win_cols), 3:4]

    def normed_copy(j):
        at = pl.ds(pl.multiple_of(j * rows, rows), rows)
        return pltpu.make_async_copy(normed.at[at], normed_out.at[at], out_sem.at[0, j])

    def qkv_copy(j):
        at = pl.ds(pl.multiple_of(j * rows, rows), rows)
        return pltpu.make_async_copy(qkv.at[:, at], qkv_out.at[:, at], out_sem.at[1, j])

    def att_keep(j):
        at = pl.ds(pl.multiple_of(j * rows, rows), rows)
        return pltpu.make_async_copy(att.at[:, at], att_out.at[:, at], out_sem.at[2, j])

    def att_copy(to):
        return pltpu.make_async_remote_copy(
            src_ref=att_send.at[to],
            dst_ref=att_land.at[z],
            send_sem=att_send_sem.at[lax.rem(to - z + nz, nz)],
            recv_sem=att_recv_sem.at[lax.rem(to - z + nz, nz)],
            device_id=(dp, to),
            device_id_type=MESH,
        )

    def project(j):
        at = pl.ds(pl.multiple_of(j * rows, rows), rows)
        normed[at, :] = layer_norm(x_land[j].astype(f32), gain, offset).astype(b16)
        for p in range(3):
            part = nt(weights_t[p * win_cols : (p + 1) * win_cols, :], normed[at, :])
            if p == 0:
                part = part + bias_q
            if p == 2:
                part = part + bias_v
            wide[p * win_cols : (p + 1) * win_cols, :] = part.astype(b16)
            qkv[p * own_cols : (p + 1) * own_cols, at] = wide[
                pl.ds(p * win_cols + shift, own_cols), :
            ]
        for h in range(nh):
            keys[h, at, :] = wide[pl.ds(win_cols + shift + h * HD, HD), :].T
        tops[:, at] = jnp.full((tops.shape[0], rows), -jnp.inf, f32)
        totals[:, at] = jnp.zeros((totals.shape[0], rows), f32)
        att[:, at] = jnp.zeros((own_cols, rows), f32)
        normed_copy(j).start()
        qkv_copy(j).start()

    def pair(i, j):
        to = pl.ds(pl.multiple_of(i * rows, rows), rows)
        of = pl.ds(pl.multiple_of(j * rows, rows), rows)
        own_seg, lanes = seg_row[0:1, to], seg_lanes[of, :]
        bias[...] = jnp.concatenate(
            [
                jnp.where(lanes == own_seg[:, k : k + 128], 0.0, NEG_FILL)
                for k in range(0, rows, 128)
            ],
            axis=1,
        )
        for h in range(nh):
            query = qkv[h * HD : (h + 1) * HD, to] * jnp.bfloat16(0.125)
            score = nn(keys[h, of, :], query) + bias[...]
            top = tops[h : h + 1, to]
            new_top = jnp.maximum(top, jnp.max(score, axis=0, keepdims=True))
            weight = jnp.exp(score - new_top)
            fade = jnp.exp(top - new_top)
            tops[h : h + 1, to] = new_top
            totals[h : h + 1, to] = totals[h : h + 1, to] * fade + jnp.sum(
                weight, axis=0, keepdims=True
            )
            value = qkv[2 * own_cols + h * HD : 2 * own_cols + (h + 1) * HD, of]
            att[h * HD : (h + 1) * HD, to] = att[h * HD : (h + 1) * HD, to] * fade + nn(
                value, weight.astype(b16)
            )

    def finish(i):
        to = pl.ds(pl.multiple_of(i * rows, rows), rows)
        for h in range(nh):
            total = totals[h : h + 1, to]
            result = att[h * HD : (h + 1) * HD, to] / total
            att[h * HD : (h + 1) * HD, to] = result
            att_send[i, h * HD : (h + 1) * HD, :] = result.astype(b16)
            lse[h : h + 1, to] = tops[h : h + 1, to] + jnp.log(total)
        att_keep(i).start()

        @pl.when(i != z)
        def _():
            att_copy(i).start()

    def take(c, low, high, last):
        project(c)

        def old_queries(f, carry):
            pair(f, c)

            @pl.when(last)
            def _():
                finish(f)

            return carry

        def new_queries(f, carry):
            pair(c, f)
            return carry

        lax.fori_loop(low, high, old_queries, 0)
        lax.fori_loop(low, high, new_queries, 0)
        pair(c, c)

        @pl.when(last)
        def _():
            finish(c)

    project(z)
    pair(z, z)
    final = jnp.maximum(z, nz - 1 - z)

    def arrivals(step, carry):
        @pl.when(z - step >= 0)
        def _():
            x_to_right(step).wait_recv()

        @pl.when(z + step <= nz - 1)
        def _():
            x_to_left(step).wait_recv()

        @pl.when(step < nz - 1)
        def _():
            x_start(step)

        high = jnp.minimum(z + step, nz)

        @pl.when(z - step >= 0)
        def _():
            take(z - step, z - step + 1, high, (step == final) & (z + step > nz - 1))

        @pl.when(z + step <= nz - 1)
        def _():
            take(z + step, jnp.maximum(z - step, 0), high, step == final)

        @pl.when(step == 1)
        def _():
            plane_step(third, 0)
            for t in range(1, steps):
                plane_step(second, t)

        @pl.when(step == 2)
        def _():
            for t in range(1, steps):
                plane_step(third, t)

        return carry

    lax.fori_loop(1, nz, arrivals, 0)
    own_keep = pltpu.make_async_copy(att_send.at[z], att_land.at[z], x_sem)
    own_keep.start()
    for s in second + third:
        s.core_wait()
    own_keep.wait()
    for off in range(1, nz):
        att_copy(lax.rem(z + off, nz)).wait()
    for j in range(nz):
        normed_copy(j).wait()
        qkv_copy(j).wait()
        att_keep(j).wait()
    for step in range(nz - 1):

        @pl.when((z < nz - 1) & (z - step >= 0))
        def _():
            x_to_right(step).wait_send()

        @pl.when((z > 0) & (z + step <= nz - 1))
        def _():
            x_to_left(step).wait_send()

    for s in spreads:
        s.sends_wait()


def forward_call(x, vec, joint, wo, wa, w1, w2, seg_row, nd, nz, nh, cid):
    rows, width = x.shape
    seq, own_cols = rows * nz, nh * HD
    win_cols = -(-(own_cols + HD) // 128) * 128
    own = joint.shape[0]
    f32, b16 = jnp.float32, jnp.bfloat16
    S = jax.ShapeDtypeStruct
    na = 6
    return pl.pallas_call(
        functools.partial(forward_kernel, nd, nz, nh),
        out_shape=(
            S((16, width), f32),
            S((nd, nz) + joint.shape, b16),
            S((nd, nz) + wo.shape, b16),
            S((nd, nz) + wa.shape, b16),
            S((nd, w1.shape[0], nz * w1.shape[1]), b16),
            S((nd, w2.shape[0], nz * w2.shape[1]), b16),
            S((seq, width), b16),
            S((3 * own_cols, seq), b16),
            S((own_cols, seq), f32),
            S((8, seq), f32),
            S((nz, own_cols, rows), b16),
        ),
        in_specs=[ANY] + [VM] * 7,
        out_specs=(VM,) + (ANY,) * 8 + (VM, ANY),
        scratch_shapes=[
            pltpu.VMEM((nz, rows, width), b16),
            pltpu.VMEM((nd, nz) + vec.shape, b16),
            pltpu.VMEM((nd, nz, own, 3 * win_cols), b16),
            pltpu.VMEM((width, vec.shape[1]), f32),
            pltpu.VMEM((width, 3 * win_cols), f32),
            pltpu.VMEM((3 * win_cols, width), b16),
            pltpu.VMEM((3 * win_cols, rows), b16),
            pltpu.VMEM((seq, width), b16),
            pltpu.VMEM((3 * own_cols, seq), b16),
            pltpu.VMEM((own_cols, seq), f32),
            pltpu.VMEM((nh, seq, HD), b16),
            pltpu.VMEM((rows, rows), f32),
            pltpu.VMEM((seq, 128), jnp.int32),
            pltpu.VMEM((8, seq), f32),
            pltpu.VMEM((8, seq), f32),
            pltpu.VMEM((nz, own_cols, rows), b16),
            pltpu.SemaphoreType.DMA((na,)),
            pltpu.SemaphoreType.DMA((na, nz)),
            pltpu.SemaphoreType.DMA((na, nz)),
            pltpu.SemaphoreType.DMA((na, nz)),
            pltpu.SemaphoreType.DMA((na, 2, nd)),
            pltpu.SemaphoreType.DMA((na, 2, nd)),
            pltpu.SemaphoreType.DMA,
            pltpu.SemaphoreType.DMA((nz,)),
            pltpu.SemaphoreType.DMA((nz,)),
            pltpu.SemaphoreType.DMA((nz,)),
            pltpu.SemaphoreType.DMA((3,)),
            pltpu.SemaphoreType.DMA((nz,)),
            pltpu.SemaphoreType.DMA((nz,)),
            pltpu.SemaphoreType.DMA((3, nz)),
        ],
        compiler_params=pltpu.CompilerParams(
            collective_id=cid, has_side_effects=True, vmem_limit_bytes=VMEM_LIMIT
        ),
    )(x, vec, joint, wo, wa, w1, w2, seg_row)


class Reduce:
    def __init__(self, slot, part, acc, land, plane, line, wide, nd, nz, dp, z, sems):
        self.slot, self.part, self.acc, self.land, self.plane, self.line = slot, part, acc, land, plane, line
        self.wide, self.nd, self.nz, self.dp, self.z = wide, nd, nz, dp, z
        self.load_sem, self.core_out, self.core_in, self.plane_out, self.plane_in, self.line_out, self.line_in = sems
        self.bits = [1 << b for b in range(1, nd.bit_length() - 1)]
        self.masks = plane_masks(self.bits, len(self.bits))
        self.cut = nz // 2
        self.cols = acc.shape[-1] // nz if wide else acc.shape[-1]

    def order(self, half):
        return self.bits if half == 0 else self.bits[::-1]

    def span(self, half):
        return (0, self.cut) if half == 0 else (self.cut, self.nz)

    def region(self, ref, i, half):
        lo, hi = self.span(half)
        if self.wide:
            return ref.at[i, :, pl.ds(lo * self.cols, (hi - lo) * self.cols)]
        return ref.at[i, pl.ds(lo, hi - lo)]

    def chunk(self, ref, i, j):
        if self.wide:
            at = j * self.cols
            at = at if isinstance(at, int) else pl.multiple_of(at, 128)
            return ref.at[i, :, pl.ds(at, self.cols)]
        return ref.at[i, j]

    def slots(self, half, step):
        order, base = self.order(half), 0
        for t in range(step):
            base += 1 << (len(order) - 1 - t)
        rest = plane_masks(order[step + 1 :], len(order) - step - 1)
        return [(m, base + k) for k, m in enumerate(rest)]

    def _load(self, m):
        return pltpu.make_async_copy(
            self.part.at[mask_flip(self.dp, m)], self.acc.at[m >> 1], self.load_sem.at[self.slot, m >> 1]
        )

    def _core(self, m):
        return pltpu.make_async_remote_copy(
            src_ref=self.part.at[mask_flip(self.dp, m ^ 1)],
            dst_ref=self.land.at[m >> 1],
            send_sem=self.core_out.at[self.slot, m >> 1],
            recv_sem=self.core_in.at[self.slot, m >> 1],
            device_id=(peer_flip(self.dp, 1), self.z),
            device_id_type=MESH,
        )

    def core_start(self):
        for m in self.masks:
            self._core(m).start()
        for m in self.masks:
            self._load(m).start()

    def _add(self, i, source, k, half):
        lo, hi = self.span(half)

        def step(j, carry):
            to, more = self.chunk(self.acc, i, j), self.chunk(source, k, j)
            to[...] = (to[...].astype(jnp.float32) + more[...].astype(jnp.float32)).astype(to.dtype)
            return carry

        lax.fori_loop(lo, hi, step, 0)

    def core_add(self):
        for m in self.masks:
            self._load(m).wait()
            self._core(m).wait_recv()
            for half in range(2):
                self._add(m >> 1, self.land, m >> 1, half)

    def _plane(self, half, step, m, place):
        bit = self.order(half)[step]
        return pltpu.make_async_remote_copy(
            src_ref=self.region(self.acc, (m ^ bit) >> 1, half),
            dst_ref=self.region(self.plane, place, half),
            send_sem=self.plane_out.at[self.slot, half, place],
            recv_sem=self.plane_in.at[self.slot, half, place],
            device_id=(peer_flip(self.dp, bit), self.z),
            device_id_type=MESH,
        )

    def plane_start(self, step):
        if step < len(self.bits):
            for half in range(2):
                for m, place in self.slots(half, step):
                    self._plane(half, step, m, place).start()

    def plane_add(self, step):
        for half in range(2):
            for m, place in self.slots(half, step):
                self._plane(half, step, m, place).wait_recv()
                self._add(m >> 1, self.plane, place, half)

    def _line(self, off):
        to = lax.rem(self.z + off, self.nz)
        return pltpu.make_async_remote_copy(
            src_ref=self.chunk(self.acc, 0, to),
            dst_ref=self.line.at[off],
            send_sem=self.line_out.at[self.slot, off],
            recv_sem=self.line_in.at[self.slot, off],
            device_id=(self.dp, to),
            device_id_type=MESH,
        )

    def line_start(self):
        for off in range(1, self.nz):
            self._line(off).start()

    def line_wait(self):
        for off in range(1, self.nz):
            self._line(off).wait_recv()

    def line_sum(self):
        self.line_wait()
        total = self.chunk(self.acc, 0, self.z)[...].astype(jnp.float32)
        for off in range(1, self.nz):
            total = total + self.line[off].astype(jnp.float32)
        return total

    def sends_wait(self):
        for m in self.masks:
            self._core(m).wait_send()
        for half in range(2):
            for step in range(len(self.bits)):
                for m, place in self.slots(half, step):
                    self._plane(half, step, m, place).wait_send()
        for off in range(1, self.nz):
            self._line(off).wait_send()


def backward_kernel(
    nd,
    nz,
    nh,
    grad_parts,
    part_wo,
    part_wa,
    part_w1,
    part_w2,
    qkv,
    att,
    lse,
    seg_row,
    normed,
    joint_full,
    x_own,
    base,
    vec_in,
    tokens_grad,
    out_joint,
    out_wo,
    out_wa,
    out_w1,
    out_w2,
    out_vec,
    grad_land,
    keys,
    values,
    key_grad,
    value_grad,
    turned,
    staged,
    rows_land,
    part_joint,
    bias_cols,
    seg_lanes,
    vec_stage,
    vec_land,
    vec_line,
    *rest,
):
    na = 5
    buffers = [rest[4 * a : 4 * a + 4] for a in range(na)]
    (
        load_sem,
        core_out,
        core_in,
        plane_out,
        plane_in,
        line_out,
        line_in,
        grad_out,
        grad_in,
        row_out,
        row_in,
        vec_out,
        vec_in_sem,
        own_sem,
    ) = rest[4 * na :]
    dp, z = lax.axis_index("dp"), lax.axis_index("mp")
    rows, width = x_own.shape
    seq = rows * nz
    own_cols = nh * HD
    f32, b16 = jnp.float32, jnp.bfloat16
    sems = (load_sem, core_out, core_in, plane_out, plane_in, line_out, line_in)
    parts = [(part_w2, True), (part_w1, True), (part_wa, False), (part_wo, False), (part_joint, False)]
    reduces = [
        Reduce(a, part, *buffers[a], wide, nd, nz, dp, z, sems) for a, (part, wide) in enumerate(parts)
    ]
    big, joint = reduces[:4], reduces[4]
    steps = len(joint.bits)

    greet(nd, nz, dp, z)

    def grad_copy(h, off):
        to = lax.rem(z + off, nz)
        return pltpu.make_async_remote_copy(
            src_ref=grad_parts.at[to, pl.ds(h * HD, HD)],
            dst_ref=grad_land.at[z, pl.ds(h * HD, HD)],
            send_sem=grad_out.at[h, off],
            recv_sem=grad_in.at[h, off],
            device_id=(dp, to),
            device_id_type=MESH,
        )

    grad_own = pltpu.make_async_copy(grad_parts.at[z], grad_land.at[z], own_sem)
    grad_own.start()
    for h in range(nh):
        for off in range(1, nz):
            grad_copy(h, off).start()
    for r in big:
        r.core_start()
    for h in range(nh):
        keys[h] = qkv[own_cols + h * HD : own_cols + (h + 1) * HD, :].T
        values[h] = qkv[2 * own_cols + h * HD : 2 * own_cols + (h + 1) * HD, :].T
    bias_cols[...] = jnp.zeros_like(bias_cols)
    seg_lanes[...] = lane_copies(seg_row)
    kc = min(512, seq)

    def row_copy(h, off):
        to = lax.rem(z + off, nz)
        return pltpu.make_async_remote_copy(
            src_ref=staged.at[to, :, pl.ds(h * HD, HD)],
            dst_ref=rows_land.at[:, z, pl.ds(h * HD, HD)],
            send_sem=row_out.at[h, off],
            recv_sem=row_in.at[h, off],
            device_id=(dp, to),
            device_id_type=MESH,
        )

    def chores(u):
        if u == 1:
            big[0].core_add()
            big[0].plane_start(0)
        if u == 2:
            big[1].core_add()
            big[1].plane_start(0)
        if u == 3:
            for r in big[2:]:
                r.core_add()
                r.plane_start(0)
        if u == 5:
            big[0].plane_add(0)
            big[0].plane_start(1)
        if u == 8:
            big[1].plane_add(0)
            big[1].plane_start(1)
        if u == 10:
            for r in big[2:]:
                r.plane_add(0)
                r.plane_start(1)

    grad_own.wait()
    for h in range(nh):
        for off in range(1, nz):
            grad_copy(h, off).wait_recv()
        key_grad[...] = jnp.zeros_like(key_grad)
        value_grad[...] = jnp.zeros_like(value_grad)

        def block(i, carry):
            start = pl.multiple_of(i * rows, rows)
            own_seg = seg_row[0:1, pl.ds(start, rows)]
            query = qkv[h * HD : (h + 1) * HD, pl.ds(start, rows)] * jnp.bfloat16(0.125)
            back = grad_land[i, h * HD : (h + 1) * HD, :]
            row_term = jnp.sum(
                back.astype(f32) * att[h * HD : (h + 1) * HD, pl.ds(start, rows)],
                axis=0,
                keepdims=True,
            )
            log_total = lse[h : h + 1, pl.ds(start, rows)]
            query_grad = jnp.zeros((HD, rows), f32)
            for c in range(0, seq, kc):
                chunk = slice(c, c + kc)
                lanes = seg_lanes[chunk, :]
                allowed = jnp.concatenate(
                    [lanes == own_seg[:, k : k + 128] for k in range(0, rows, 128)], axis=1
                )
                score = nn(keys[h, chunk, :], query)
                weight = jnp.where(allowed, jnp.exp(score - log_total), 0.0)
                value_grad[chunk, :] += nt(weight.astype(b16), back)
                weight_grad = nn(values[h, chunk, :], back)
                score_grad = (weight * (weight_grad - row_term)).astype(b16)
                key_grad[chunk, :] += nt(score_grad, query)
                query_grad = query_grad + nn(
                    qkv[own_cols + h * HD : own_cols + (h + 1) * HD, chunk], score_grad
                )
            staged[i, 0, h * HD : (h + 1) * HD, :] = (query_grad * 0.125).astype(b16)
            for b in range(nz):
                u = h * nz + b

                @pl.when(i == b)
                def _():
                    chores(u)

            return carry

        lax.fori_loop(0, nz, block, 0)
        for p, source in ((1, key_grad), (2, value_grad)):
            turned[...] = source[...].T
            for j in range(nz):
                staged[j, p, h * HD : (h + 1) * HD, :] = turned[:, j * rows : (j + 1) * rows].astype(b16)
        for off in range(1, nz):
            row_copy(h, off).start()
        rows_land[:, z, h * HD : (h + 1) * HD, :] = staged[z, :, h * HD : (h + 1) * HD, :]
        at = pl.ds(pl.multiple_of(z * own_cols + h * HD, HD), HD)
        for col, p in ((0, 0), (1, 2)):
            total = jnp.zeros((HD, 1), f32)
            for j in range(nz):
                total = total + jnp.sum(
                    staged[j, p, h * HD : (h + 1) * HD, :].astype(f32), axis=1, keepdims=True
                )
            bias_cols[at, col : col + 1] = total

    grad_t = jnp.zeros((3 * own_cols, width), f32)
    for j in range(nz):
        grad_t = grad_t + nn(
            staged[j].reshape(3 * own_cols, rows), normed[j * rows : (j + 1) * rows, :]
        )
    grad_joint = grad_t.T
    own = part_joint.shape[2]
    for d in range(nd):
        for j in range(nz):
            at = (d * nz + j) * own
            part_joint[d, j] = grad_joint[at : at + own, :].astype(b16)
    joint.core_start()
    for t in range(1, steps):
        for r in big:
            r.plane_add(t)
            r.plane_start(t + 1)
    for r in big:
        r.line_start()
    joint.core_add()
    joint.plane_start(0)
    for t in range(steps):
        joint.plane_add(t)
        joint.plane_start(t + 1)
    joint.line_start()

    for h in range(nh):
        for off in range(1, nz):
            row_copy(h, off).wait_recv()
    back_t = nn(joint_full[...], rows_land[...].reshape(3 * width, rows))
    back = back_t.T
    gain = vec_in[0:1, :]
    x = x_own[...].astype(f32)
    centre = x - jnp.mean(x, axis=-1, keepdims=True)
    inverse = lax.rsqrt(jnp.mean(centre * centre, axis=-1, keepdims=True) + EPSILON)
    unit = centre * inverse
    scaled = back * gain
    tokens_grad[...] = base[...] + inverse * (
        scaled
        - jnp.mean(scaled, axis=-1, keepdims=True)
        - unit * jnp.mean(scaled * unit, axis=-1, keepdims=True)
    )
    bias_rows = bias_cols[...].T
    vec_stage[0] = vec_in[...]
    vec_stage[0, 0:1, :] = jnp.sum(back * unit, axis=0, keepdims=True)
    vec_stage[0, 1:2, :] = jnp.sum(back, axis=0, keepdims=True)
    vec_stage[0, 2:4, :] = bias_rows[0:2, :]
    bits = [1] + joint.bits

    def vec_copy(t):
        return pltpu.make_async_remote_copy(
            src_ref=vec_stage.at[t],
            dst_ref=vec_land.at[t],
            send_sem=vec_out.at[t],
            recv_sem=vec_in_sem.at[t],
            device_id=(peer_flip(dp, bits[t]), z),
            device_id_type=MESH,
        )

    def vec_line_copy(off):
        return pltpu.make_async_remote_copy(
            src_ref=vec_stage.at[len(bits)],
            dst_ref=vec_line.at[off],
            send_sem=vec_out.at[len(bits) + off],
            recv_sem=vec_in_sem.at[len(bits) + off],
            device_id=(dp, lax.rem(z + off, nz)),
            device_id_type=MESH,
        )

    for t in range(len(bits)):
        vec_copy(t).start()
        vec_copy(t).wait_recv()
        vec_stage[t + 1] = vec_stage[t] + vec_land[t]
    for off in range(1, nz):
        vec_line_copy(off).start()
    for r, out in zip(big, (out_w2, out_w1, out_wa, out_wo)):
        out[...] = r.line_sum()
    joint.line_wait()
    out_joint[z] = joint.acc[0, z].astype(f32)
    for off in range(1, nz):
        out_joint[lax.rem(z - off + nz, nz)] = joint.line[off].astype(f32)
    total = vec_stage[len(bits)]
    for off in range(1, nz):
        vec_line_copy(off).wait_recv()
        total = total + vec_line[off]
    out_vec[...] = total
    for t in range(len(bits)):
        vec_copy(t).wait_send()
    for off in range(1, nz):
        vec_line_copy(off).wait_send()
        for h in range(nh):
            grad_copy(h, off).wait_send()
            row_copy(h, off).wait_send()
    for r in reduces:
        r.sends_wait()


def backward_call(
    grad_parts, wo, wa, w1, w2, qkv, att, lse, seg_row, normed, joint_full, x_own, base, vec_in, nd, nz, nh, cid
):
    rows, width = x_own.shape
    seq, own_cols = rows * nz, nh * HD
    own = width // (nd * nz)
    f32, b16 = jnp.float32, jnp.bfloat16
    S, D = jax.ShapeDtypeStruct, pltpu.SemaphoreType.DMA
    joint_shape = (nd, nz, own, 3 * own_cols)
    held = []
    for shape, wide in ((w2.shape, True), (w1.shape, True), (wa.shape, False), (wo.shape, False), (joint_shape, False)):
        piece = shape[1:]
        line = (nz, piece[0], piece[1] // nz) if wide else piece
        held += [
            pltpu.VMEM((nd // 2,) + piece, b16),
            pltpu.VMEM((nd // 2,) + piece, b16),
            pltpu.VMEM((max(nd // 2 - 1, 1),) + piece, b16),
            pltpu.VMEM(line, b16),
        ]
    na, nb = 5, nd.bit_length() - 1
    return pl.pallas_call(
        functools.partial(backward_kernel, nd, nz, nh),
        out_shape=(
            S((rows, width), f32),
            S((nz, own, 3 * own_cols), f32),
            S(wo.shape[2:], f32),
            S(wa.shape[2:], f32),
            S((w1.shape[1], w1.shape[2] // nz), f32),
            S((w2.shape[1], w2.shape[2] // nz), f32),
            S(vec_in.shape, f32),
        ),
        in_specs=[ANY] * 5 + [VM] * 9,
        out_specs=(VM,) * 7,
        scratch_shapes=[
            pltpu.VMEM((nz, own_cols, rows), b16),
            pltpu.VMEM((nh, seq, HD), b16),
            pltpu.VMEM((nh, seq, HD), b16),
            pltpu.VMEM((seq, HD), f32),
            pltpu.VMEM((seq, HD), f32),
            pltpu.VMEM((HD, seq), f32),
            pltpu.VMEM((nz, 3, own_cols, rows), b16),
            pltpu.VMEM((3, nz, own_cols, rows), b16),
            pltpu.VMEM(joint_shape, b16),
            pltpu.VMEM((width, 128), f32),
            pltpu.VMEM((seq, 128), jnp.int32),
            pltpu.VMEM((nb + 1,) + vec_in.shape, f32),
            pltpu.VMEM((nb,) + vec_in.shape, f32),
            pltpu.VMEM((nz,) + vec_in.shape, f32),
        ]
        + held
        + [
            D((na, nd // 2)),
            D((na, nd // 2)),
            D((na, nd // 2)),
            D((na, 2, nd // 2)),
            D((na, 2, nd // 2)),
            D((na, nz)),
            D((na, nz)),
            D((nh, nz)),
            D((nh, nz)),
            D((nh, nz)),
            D((nh, nz)),
            D((nb + nz,)),
            D((nb + nz,)),
            D,
        ],
        compiler_params=pltpu.CompilerParams(
            collective_id=cid, has_side_effects=True, vmem_limit_bytes=60 << 20
        ),
    )(grad_parts, wo, wa, w1, w2, qkv, att, lse, seg_row, normed, joint_full, x_own, base, vec_in)


def gelu_pair(u):
    size = jnp.abs(u)
    t = 1.0 / (1.0 + (0.3275911 * 0.7071067811865476) * size)
    poly = ((((1.061405429 * t - 1.453152027) * t + 1.421413741) * t - 0.284496736) * t + 0.254829592) * t
    bell = jnp.exp(-0.5 * u * u)
    tail = 0.5 * poly * bell
    share = jnp.where(u >= 0.0, 1.0 - tail, tail)
    return u * share, share + u * (0.3989422804014327 * bell)


def norm_parts(values):
    centre = values - jnp.mean(values, axis=-1, keepdims=True)
    inverse = lax.rsqrt(jnp.mean(centre * centre, axis=-1, keepdims=True) + EPSILON)
    return centre * inverse, inverse


def norm_back(grad, unit, inverse, gain):
    scaled = grad * gain
    back = inverse * (
        scaled
        - jnp.mean(scaled, axis=-1, keepdims=True)
        - unit * jnp.mean(scaled * unit, axis=-1, keepdims=True)
    )
    return (
        back,
        jnp.sum(grad * unit, axis=0, keepdims=True),
        jnp.sum(grad, axis=0, keepdims=True),
    )


def middle_kernel(
    pieces,
    nz,
    al_in,
    x_in,
    og_in,
    ag_in,
    wo_in,
    wa_in,
    w1_in,
    w2_in,
    vec,
    expand_bias,
    align_bias,
    block_out,
    align_out,
    base,
    grad_parts,
    part_wo,
    part_wa,
    part_w1,
    part_w2,
    sums,
    al,
    x,
    og,
    ag,
    wo,
    wa,
    w1,
    w2,
    act,
    slope,
    block,
    align,
    base_v,
    grads,
    own_wo,
    own_wa,
    own_w1,
    own_w2,
    load_sem,
    store_sem,
):
    f32, b16 = jnp.float32, jnp.bfloat16
    width = x.shape[1]
    hidden = w1.shape[1]
    step = hidden // pieces
    cols = [slice(j * step, (j + 1) * step) for j in range(pieces)]
    loads = {}

    def load(name, source, to):
        loads[name] = pltpu.make_async_copy(source, to, load_sem.at[len(loads)])
        loads[name].start()

    load("wo", wo_in, wo)
    load("al", al_in, al)
    load("x", x_in, x)
    for j in range(pieces):
        load(("w1", j), w1_in.at[:, cols[j]], w1.at[:, cols[j]])
        load(("w2", j), w2_in.at[:, cols[j]], w2.at[:, cols[j]])
    load("wa", wa_in, wa)
    load("ag", ag_in, ag)
    load("og", og_in, og)
    stores = []

    def store(source, to):
        stores.append(pltpu.make_async_copy(source, to, store_sem.at[len(stores)]))
        stores[-1].start()

    def row(i):
        return vec[i : i + 1, :]

    sums[...] = jnp.zeros_like(sums)
    sums[0:1, :] = row(0)
    for name in ("wo", "al", "x"):
        loads[name].wait()
    x1 = x[...].astype(f32) + nn(al[...].T, wo[...]) + row(4)
    unit_two, inverse_two = norm_parts(x1)
    n2 = (unit_two * row(5) + row(6)).astype(b16)
    y = x1 + row(7)
    for j in range(pieces):
        loads["w1", j].wait()
        u = nn(n2, w1[:, cols[j]]) + expand_bias[:, cols[j]]
        value, derivative = gelu_pair(u)
        act[:, cols[j]] = value.astype(b16)
        slope[:, cols[j]] = derivative.astype(b16)
    for j in range(pieces):
        loads["w2", j].wait()
        y = y + nt(act[:, cols[j]], w2[:, cols[j]])
    block[...] = y.astype(b16)
    store(block, block_out)
    unit_three, inverse_three = norm_parts(y)
    n3 = (unit_three * row(8) + row(9)).astype(b16)
    loads["wa"].wait()
    loads["ag"].wait()
    align[...] = (nn(n3, wa[...]) + align_bias[...]).astype(b16)
    store(align, align_out)
    own_wa[...] = nn(n3.T, ag[...]).astype(b16)
    store(own_wa, part_wa)
    aligned = jnp.sum(ag[...].astype(f32), axis=0, keepdims=True)
    done = 0
    at = 10 + hidden // width
    while done < aligned.shape[1]:
        size = min(width, aligned.shape[1] - done)
        sums[at : at + 1, 0:size] = aligned[:, done : done + size]
        done, at = done + size, at + 1
    back, sums[8:9, :], sums[9:10, :] = norm_back(
        nt(ag[...], wa[...]), unit_three, inverse_three, row(8)
    )
    loads["og"].wait()
    gy = og[...].astype(f32) + back
    gm = gy.astype(b16)
    sums[7:8, :] = jnp.sum(gm.astype(f32), axis=0, keepdims=True)
    gm_t, n2_t = gm.T, n2.T
    gn2 = jnp.zeros(gy.shape, f32)
    for j in range(pieces):
        own_w2[:, cols[j]] = nn(gm_t, act[:, cols[j]]).astype(b16)
        store(own_w2.at[:, cols[j]], part_w2.at[:, cols[j]])
        gu = (nn(gm, w2[:, cols[j]]) * slope[:, cols[j]].astype(f32)).astype(b16)
        slope[:, cols[j]] = gu
        total = jnp.sum(gu.astype(f32), axis=0, keepdims=True)
        for k in range(0, step, width):
            at = (j * step + k) // width
            sums[10 + at : 11 + at, (j * step + k) % width : (j * step + k) % width + min(step, width)] = (
                total[:, k : k + width]
            )
        gn2 = gn2 + nt(gu, w1[:, cols[j]])
    back, sums[5:6, :], sums[6:7, :] = norm_back(gn2, unit_two, inverse_two, row(5))
    gx1 = gy + back
    base_v[...] = gx1
    store(base_v, base)
    go = gx1.astype(b16)
    sums[4:5, :] = jnp.sum(go.astype(f32), axis=0, keepdims=True)
    grads[...] = nt(wo[...], go).astype(b16)
    store(grads, grad_parts)
    for j in range(pieces):
        own_w1[:, cols[j]] = nn(n2_t, slope[:, cols[j]]).astype(b16)
        store(own_w1.at[:, cols[j]], part_w1.at[:, cols[j]])
    own_wo[...] = nn(al[...], go).astype(b16)
    store(own_wo, part_wo)
    for s in stores:
        s.wait()


def middle_call(al, x, og, ag, wo, wa, w1, w2, vec, expand_bias, align_bias, nz):
    f32, b16 = jnp.float32, jnp.bfloat16
    S = jax.ShapeDtypeStruct
    rows, width = x.shape
    hidden, wide = w1.shape[1], wa.shape[1]
    pieces = 4
    shapes = [al, x, og, ag, wo, wa, w1, w2]
    return pl.pallas_call(
        functools.partial(middle_kernel, pieces, nz),
        out_shape=(
            S((rows, width), b16),
            S((rows, wide), b16),
            S((rows, width), f32),
            S((width, rows), b16),
            S(wo.shape, b16),
            S(wa.shape, b16),
            S(w1.shape, b16),
            S(w2.shape, b16),
            S(vec.shape, f32),
        ),
        in_specs=[ANY] * 8 + [VM] * 3,
        out_specs=(ANY,) * 8 + (VM,),
        scratch_shapes=[pltpu.VMEM(a.shape, b16) for a in shapes]
        + [
            pltpu.VMEM((rows, hidden), b16),
            pltpu.VMEM((rows, hidden), b16),
            pltpu.VMEM((rows, width), b16),
            pltpu.VMEM((rows, wide), b16),
            pltpu.VMEM((rows, width), f32),
            pltpu.VMEM((width, rows), b16),
            pltpu.VMEM(wo.shape, b16),
            pltpu.VMEM(wa.shape, b16),
            pltpu.VMEM(w1.shape, b16),
            pltpu.VMEM(w2.shape, b16),
            pltpu.SemaphoreType.DMA((6 + 2 * pieces,)),
            pltpu.SemaphoreType.DMA((6 + 2 * pieces,)),
        ],
        compiler_params=pltpu.CompilerParams(vmem_limit_bytes=60 << 20),
    )(al, x, og, ag, wo, wa, w1, w2, vec, expand_bias, align_bias)


def local(
    tokens,
    segments,
    out_grad,
    align_grad,
    first_gain,
    first_shift,
    joint_weight,
    query_bias,
    value_bias,
    output_weight,
    output_bias,
    second_gain,
    second_shift,
    expand_bias,
    reduce_bias,
    head_gain,
    head_shift,
    align_weight,
    align_bias,
    expand_weight,
    reduce_weight,
):
    nd, nz = lax.axis_size("dp"), lax.axis_size("mp")
    n = nd * nz
    z = lax.axis_index("mp")
    rows, width = tokens.shape
    seq = rows * nz
    nh = H // nz
    own_cols = nh * HD
    f32, b16 = jnp.float32, jnp.bfloat16

    own = first_gain.shape[0]

    small = (
        first_gain,
        first_shift,
        query_bias,
        value_bias,
        output_bias,
        second_gain,
        second_shift,
        reduce_bias,
        head_gain,
        head_shift,
        expand_bias,
        align_bias,
    )
    flat, at = 0.0, 0
    for v in small:
        flat = flat + jnp.pad(v, (at, 16 * own - at - v.shape[0]))
        at += v.shape[0]
    vec = jnp.pad(flat.reshape(16, own).T, ((0, 0), (0, 112)))
    seg_row = segments.reshape(1, seq)
    vectors, joint_full, wo, wa, w1, w2, normed_all, qkv, att, lse, attended = forward_call(
        tokens,
        vec,
        joint_weight,
        output_weight,
        align_weight,
        expand_weight,
        reduce_weight.T,
        seg_row,
        nd,
        nz,
        nh,
        1,
    )
    joint_full = joint_full.reshape(width, 3 * width)
    output_full = wo.reshape(width, width)
    align_full = wa.reshape(width, -1)
    expand_full = w1.reshape(width, -1)
    reduce_full = w2.reshape(width, -1)
    attended = attended.reshape(width, rows)
    count = -(-expand_bias.shape[0] // own)
    bias_expand = (
        vectors[10 : 10 + count].reshape(count, n, own).transpose(1, 0, 2).reshape(n, count * own)
    )[:, : expand_bias.shape[0]].reshape(-1)
    count_align = -(-align_bias.shape[0] // own)
    bias_align = (
        vectors[10 + count : 10 + count + count_align]
        .reshape(count_align, n, own)
        .transpose(1, 0, 2)
        .reshape(n, count_align * own)
    )[:, : align_bias.shape[0]].reshape(-1)

    block_out, align_out, base, grad_parts, p_wo, p_wa, p_w1, p_w2, vec_in = middle_call(
        attended,
        tokens,
        out_grad,
        align_grad,
        output_full,
        align_full,
        expand_full,
        reduce_full,
        vectors,
        bias_expand[None],
        bias_align[None],
        nz,
    )
    hidden = expand_full.shape[1]
    tokens_grad, joint_mine, g_wo, g_wa, g_w1, g_w2, sums = backward_call(
        grad_parts.reshape(nz, own_cols, rows),
        p_wo.reshape(nd, nz, own, width),
        p_wa.reshape(nd, nz, own, -1),
        p_w1.reshape(nd, width // nd, hidden),
        p_w2.reshape(nd, width // nd, hidden),
        qkv,
        att,
        lse,
        seg_row,
        normed_all,
        joint_full,
        tokens,
        base,
        vec_in,
        nd,
        nz,
        nh,
        2,
    )
    g_joint = (
        joint_mine.reshape(nz, own, 3, own_cols).transpose(1, 2, 0, 3).reshape(own, 3 * width)
    )
    me = lax.axis_index("dp") * nz + z
    mine = lax.dynamic_slice_in_dim(sums[:10], me * own, own, axis=1)
    flat = sums[10:].reshape(-1)
    size_e, size_a = expand_bias.shape[0], align_bias.shape[0]
    g_expand_b = lax.dynamic_slice_in_dim(flat, me * size_e, size_e)
    g_align_b = lax.dynamic_slice_in_dim(flat, hidden + me * size_a, size_a)
    return (
        block_out,
        align_out,
        tokens_grad,
        mine[0],
        mine[1],
        g_joint,
        mine[2],
        mine[3],
        g_wo,
        mine[4],
        mine[5],
        mine[6],
        g_expand_b,
        mine[7],
        mine[8],
        mine[9],
        g_wa,
        g_align_b,
        g_w1,
        g_w2.T,
    )


def solution(mesh):
    both = P(("dp", "mp"))
    rows = P(("dp", "mp"), None)
    in_specs = (
        (rows, P("dp", None), rows, rows, both, both, rows, both, both, rows)
        + (both,) * 7
        + (rows, both, P("dp", "mp"), P("mp", "dp"))
    )
    out_specs = (
        (rows, rows, rows, both, both, rows, both, both, rows)
        + (both,) * 7
        + (rows, both, P("dp", "mp"), P("mp", "dp"))
    )
    return jax.shard_map(local, mesh=mesh, in_specs=in_specs, out_specs=out_specs, check_vma=False)
```

profile of v0, /device:TPU:0, one launch (start us, length us, event | category | flops | bytes accessed | tf_op | source)
XLA Modules:
  0.0 288.2 jit_solution(9579248302044921445)
XLA Ops:
  0.7 0.9 pad_add_fusion
  1.5 0.1 reshape.94
  1.6 0.1 copy.48
  1.7 0.6 pad.64.vec_own
  2.3 120.2 %shard_map.356 = (f32[16,768]{1,0:T(8,128)}, bf16[8,4,24,2304]{3,2,1,0:T(8,128)(2,1)}, bf16[8,4,24,768]{3,2,1,0:T(8,128)(2,1)}, bf16[8,4,24,1024]{3,2,1,0:T(8,12...) custom-call(bf16[512,768]{1,0:T(8,128)(2,1)} %x_own.3, ...), custom_call_target="tpu_custom_call" | custom-call | tf_op jit(solution)/shard_map/pallas_call | solution.py:593
  122.5 0.7 slice.45
  123.3 0.1 reshape.100
  123.4 0.7 broadcast_in_dim_reshape_reshape.3.expand_bias
  124.2 0.7 slice.46
  124.9 0.1 reshape.101
  125.1 0.7 broadcast_in_dim_reshape.3.align_bias
  125.8 34.5 %shard_map.357 = (bf16[512,768]{1,0:T(8,128)(2,1)}, bf16[512,1024]{1,0:T(8,128)(2,1)}, f32[512,768]{1,0:T(8,128)}, bf16[768,512]{1,0:T(8,128)(2,1)}, bf16[768,76...) custom-call(bf16[768,512]{1,0:T(8,128)(2,1)} %bitcast.49, ...), custom_call_target="tpu_custom_call" | custom-call | tf_op jit(solution)/shard_map/pallas_call | solution.py:1325
  160.3 119.4 %shard_map.358 = (f32[512,768]{1,0:T(8,128)}, f32[4,24,576]{2,1,0:T(8,128)}, f32[24,768]{1,0:T(8,128)}, f32[24,1024]{1,0:T(8,128)}, f32[96,768]{1,0:T(8,128)}, /*index=5*/f32[96,768]{1,0:T(8,128)}, f32[16,768]{1,0:T(8,128)}) custom-call(bf16[4,192,512]{2,1,0:T(8,128)(2,1)} %bitcast.50, bf16[8,4,24,768]{3,2,1,0:T(8,128)(2,1)} %bitcast.48, ...), custom_call_target="tpu_custom_call" | custom-call | tf_op jit(solution)/shard_map/pallas_call | solution.py:1091
  279.7 1.2 reshape.109
  281.0 0.2 copy.52
  281.2 0.9 reshape.110
  282.1 0.6 dynamic_slice.11
  282.7 0.6 dynamic_slice.10
  283.3 0.6 dynamic-slice_bitcast_fusion
  283.9 1.1 copy.58
  285.1 0.6 copy.59
  285.7 0.6 copy.60
  286.4 0.7 copy.61
  287.1 0.7 copy.62
  (18 shorter events, 0.2 us)
Async XLA Ops:
  279.7 2.3 copy-start.5
  279.7 4.2 %copy-start = (f32[512,768]{1,0:T(8,128)S(1)}, f32[512,768]{1,0:T(8,128)}, u32[]{:S(2)}) copy-start(f32[512,768]{1,0:T(8,128)} %get-tuple-element.106) | copy-start | bytes 4718596
  283.9 1.2 copy-start.4
  283.9 1.8 copy-start.3
  283.9 2.4 copy-start.2
  283.9 3.2 %copy-start.1 = (f32[96,768]{1,0:T(8,128)S(1)}, f32[96,768]{1,0:T(8,128)}, u32[]{:S(2)}) copy-start(f32[96,768]{1,0:T(8,128)} %get-tuple-element.73) | copy-start | bytes 884740
where the time goes:
time: 292 us; the launch traced here: 288 us
  Pallas kernels  274 us (94%)
  local copies, waits for them, and re-layouts  12 us (4%)
    pallas_call x1, Pallas kernels, forward_call(): pl.pallas_call(functools.partial(forward_kernel, nd, nz, nh), out_shape=(...  120 us
    pallas_call x1, Pallas kernels, backward_call(): pl.pallas_call(functools.partial(backward_kernel, nd, nz, nh), out_shape=...  119 us
    pallas_call x1, Pallas kernels, middle_call(): pl.pallas_call(functools.partial(middle_kernel, pieces, nz), out_shape=(S...  34.5 us

commit v1 on v0

--- a/solution.py
+++ b/solution.py
@@ -176,7 +176,7 @@
             for mask in plane_masks(self.bits, len(self.bits)):
                 self._arrival(half, mask ^ 1, 1).wait_recv()
 
-    def sends_wait(self):
+    def line_sends_wait(self):
         for step in range(self.nz - 1):
 
             @pl.when((self.z < self.nz - 1) & (self.z - step >= 0))
@@ -187,6 +187,7 @@
             def _():
                 self._left(step).wait_send()
 
+    def plane_sends_wait(self):
         for half in range(2):
             order = self.order(half)
             for step in range(len(self.bits)):
@@ -196,35 +197,69 @@
                 self._plane(half, mask, 1).wait_send()
 
 
-def greet(nd, nz, dp, z, line=True, plane=True):
+def greet(nd, nz, dp, z, everyone=False):
     barrier = pltpu.get_barrier_semaphore()
     count = 0
-    if line:
-        for off in range(1, nz):
-            pl.semaphore_signal(
-                barrier, inc=1, device_id=(dp, lax.rem(z + off, nz)), device_id_type=MESH
-            )
-            count += 1
-    if plane:
-        bit = 1
-        while bit < nd:
-            pl.semaphore_signal(
-                barrier, inc=1, device_id=(peer_flip(dp, bit), z), device_id_type=MESH
-            )
-            count += 1
-            bit *= 2
+    for off in range(1, nz):
+        pl.semaphore_signal(
+            barrier, inc=1, device_id=(dp, lax.rem(z + off, nz)), device_id_type=MESH
+        )
+        count += 1
+    bits = [1 << b for b in range(nd.bit_length() - 1)]
+    peers = (
+        [lax.rem(dp + off, nd) for off in range(1, nd)]
+        if everyone
+        else [peer_flip(dp, bit) for bit in bits]
+    )
+    for peer in peers:
+        pl.semaphore_signal(barrier, inc=1, device_id=(peer, z), device_id_type=MESH)
+        count += 1
     pl.semaphore_wait(barrier, count)
 
 
 def lane_copies(seg_row):
     return jnp.broadcast_to(seg_row[...], (128, seg_row.shape[1])).T
+
+
+def gelu_pair(u):
+    size = jnp.abs(u)
+    t = 1.0 / (1.0 + (0.3275911 * 0.7071067811865476) * size)
+    poly = ((((1.061405429 * t - 1.453152027) * t + 1.421413741) * t - 0.284496736) * t + 0.254829592) * t
+    bell = jnp.exp(-0.5 * u * u)
+    tail = 0.5 * poly * bell
+    share = jnp.where(u >= 0.0, 1.0 - tail, tail)
+    return u * share, share + u * (0.3989422804014327 * bell)
+
+
+def norm_parts(values):
+    centre = values - jnp.mean(values, axis=-1, keepdims=True)
+    inverse = lax.rsqrt(jnp.mean(centre * centre, axis=-1, keepdims=True) + EPSILON)
+    return centre * inverse, inverse
+
+
+def norm_back(grad, unit, inverse, gain):
+    scaled = grad * gain
+    back = inverse * (
+        scaled
+        - jnp.mean(scaled, axis=-1, keepdims=True)
+        - unit * jnp.mean(scaled * unit, axis=-1, keepdims=True)
+    )
+    return (
+        back,
+        jnp.sum(grad * unit, axis=0, keepdims=True),
+        jnp.sum(grad, axis=0, keepdims=True),
+    )
 
 
 def forward_kernel(
     nd,
     nz,
     nh,
+    size_e,
+    size_a,
     x_own,
+    og_in,
+    ag_in,
     vec_own,
     joint_own,
     wo_own,
@@ -232,21 +267,31 @@
     w1_own,
     w2_own,
     seg_row,
-    vec_rows,
+    block_out,
+    align_out,
+    base_out,
+    grads_out,
+    part_wo,
+    part_wa,
+    part_w1,
+    part_w2,
+    sums,
     joint,
-    wo,
-    wa,
-    w1,
-    w2,
+    wo_land,
+    wa_land,
     normed_out,
     qkv_out,
     att_out,
     lse,
-    att_land,
+    al_land,
     x_land,
     vec,
     window,
+    w1,
+    w2,
     vec_cols,
+    vec_rows,
+    bias_rows,
     weights,
     weights_t,
     wide,
@@ -259,6 +304,16 @@
     tops,
     totals,
     att_send,
+    og,
+    ag,
+    wo,
+    wa,
+    act,
+    slope,
+    block,
+    align,
+    base,
+    grads,
     keep_sem,
     right_sem,
     left_sem,
@@ -269,31 +324,44 @@
     x_right,
     x_left,
     x_recv,
-    win_sem,
+    win_send,
+    win_recv,
     att_send_sem,
     att_recv_sem,
     out_sem,
+    load_sem,
+    store_sem,
 ):
     dp, z = lax.axis_index("dp"), lax.axis_index("mp")
     rows, width = x_own.shape
     seq = rows * nz
+    own = vec_own.shape[0]
     own_cols = nh * HD
     win_cols = window.shape[-1] // 3
     win = z * own_cols // 128 * 128
     shift = pl.multiple_of(z * own_cols - win, HD)
     win = pl.multiple_of(win, 128)
+    hidden, aligned = size_e * nd * nz, size_a * nd * nz
     f32, b16 = jnp.float32, jnp.bfloat16
     sems = (keep_sem, right_sem, left_sem, line_sem, send_sem, recv_sem)
     specs = [
         (vec_own, vec, False),
         (joint_own, joint, False),
-        (wo_own, wo, False),
+        (wo_own, wo_land, False),
         (w1_own, w1, True),
-        (wa_own, wa, False),
         (w2_own, w2, True),
+        (wa_own, wa_land, False),
+        (joint_own, window, False),
     ]
     spreads = [Spread(i, *spec, nd, nz, dp, z, sems) for i, spec in enumerate(specs)]
-    first, second, third = spreads[:2], spreads[2:4], spreads[4:]
+    vecs, joints, early, late, heads = (
+        spreads[:1],
+        spreads[1:2],
+        spreads[2:5],
+        spreads[5:6],
+        spreads[6:],
+    )
+    lined = spreads[:6]
     steps = len(spreads[0].bits)
 
     def line_step(group, step):
@@ -344,69 +412,99 @@
         def _():
             x_to_left(step).start()
 
-    greet(nd, nz, dp, z)
-    for s in spreads:
-        s.keep().start()
+    def piece(to, p):
+        at = to * own_cols // 128 * 128 + p * width
+        return joint_own.at[:, pl.ds(pl.multiple_of(at, 128), win_cols)]
+
+    def piece_copy(off, p):
+        to = lax.rem(z + off, nz)
+        return pltpu.make_async_remote_copy(
+            src_ref=piece(to, p),
+            dst_ref=window.at[dp, z, :, pl.ds(p * win_cols, win_cols)],
+            send_sem=win_send.at[off, p],
+            recv_sem=win_recv.at[off, p],
+            device_id=(dp, to),
+            device_id_type=MESH,
+        )
+
+    def piece_keep(p):
+        return pltpu.make_async_copy(
+            piece(z, p), window.at[dp, z, :, pl.ds(p * win_cols, win_cols)], win_send.at[0, p]
+        )
+
+    og_load = pltpu.make_async_copy(og_in, og, load_sem.at[0])
+    ag_load = pltpu.make_async_copy(ag_in, ag, load_sem.at[1])
     x_keep = pltpu.make_async_copy(x_own, x_land.at[z], x_sem)
     x_keep.start()
-    for s in first:
+    greet(nd, nz, dp, z)
+    for s in lined:
+        s.keep().start()
+    for s in vecs:
         s.line_start(0)
+    for off in range(1, nz):
+        for p in range(3):
+            piece_copy(off, p).start()
+    for p in range(3):
+        piece_keep(p).start()
+    for s in early:
+        s.line_start(0)
+    og_load.start()
+    ag_load.start()
     for step in range(1, nz - 1):
-        line_step(first, step)
-    for s in second:
-        s.line_start(0)
+        line_step(vecs, step)
     seg_lanes[...] = lane_copies(seg_row)
-    line_step(first, nz - 1)
-    plane_open(first)
-    line_step(second, 1)
-    plane_step(first, 0)
+    for p in range(3):
+        piece_keep(p).wait()
+        for off in range(1, nz):
+            piece_copy(off, p).wait_recv()
+    for s in heads:
+        s.plane_start(0)
+        s.core_start(-1)
+    line_step(vecs, nz - 1)
+    plane_open(vecs)
+    line_step(early, 1)
+    plane_step(heads + vecs, 0)
     for step in range(2, nz - 1):
-        line_step(second, step)
-    for s in third:
-        s.line_start(0)
-    line_step(second, nz - 1)
-    plane_open(second)
-    line_step(third, 1)
-    for t in range(1, steps):
-        plane_step(first, t)
-    for step in range(2, nz - 1):
-        line_step(third, step)
+        line_step(early, step)
     x_keep.wait()
     x_start(0)
-    line_step(third, nz - 1)
-    plane_open(third)
-    plane_step(second, 0)
-    for s in first:
+    line_step(early, nz - 1)
+    plane_open(early)
+    for t in range(1, steps):
+        plane_step(heads + vecs, t)
+    for s in heads + vecs:
         s.core_wait()
 
-    loads = []
-    for p in range(3):
-        load = pltpu.make_async_copy(
-            joint.at[:, :, :, pl.ds(pl.multiple_of(p * width + win, 128), win_cols)],
-            window.at[:, :, :, pl.ds(p * win_cols, win_cols)],
-            win_sem.at[p],
-        )
-        load.start()
-        loads.append(load)
-    own = vec.shape[2]
     for d in range(nd):
         for j in range(nz):
             at = (d * nz + j) * own
             vec_cols[at : at + own, :] = vec[d, j].astype(f32)
-    vec_t = vec_cols[...].T
-    vec_rows[...] = vec_t[: vec_rows.shape[0]]
-    for load in loads:
-        load.wait()
-    for d in range(nd):
-        for j in range(nz):
-            at = (d * nz + j) * own
             weights[at : at + own, :] = window[d, j].astype(f32)
+    vec_rows[...] = vec_cols[...].T[: vec_rows.shape[0]]
     for p in range(3):
         cols = slice(p * win_cols, (p + 1) * win_cols)
         weights_t[cols, :] = weights[:, cols].T.astype(b16)
-    gain, offset = vec_rows[0:1, :], vec_rows[1:2, :]
+
+    def row(i):
+        return vec_rows[i : i + 1, :]
+
     bias_q = vec_cols[pl.ds(win, win_cols), 2:3]
     bias_v = vec_cols[pl.ds(win, win_cols), 3:4]
+
+    def flatten(source, to):
+        cols = to.shape[1]
+        part = cols // -(-cols // window.shape[-1])
+        for k in range(0, cols, part):
+            load = pltpu.make_async_copy(
+                source.at[:, :, :, pl.ds(k, part)], window.at[:, :, :, pl.ds(0, part)], load_sem.at[2]
+            )
+            load.start()
+            load.wait()
+            for d in range(nd):
+                for j in range(nz):
+                    at = (d * nz + j) * own
+                    weights[at : at + own, :part] = window[d, j, :, :part].astype(f32)
+            to[:, k : k + part] = weights[:, :part].astype(b16)
 
     def normed_copy(j):
         at = pl.ds(pl.multiple_of(j * rows, rows), rows)
@@ -423,7 +521,7 @@
     def att_copy(to):
         return pltpu.make_async_remote_copy(
             src_ref=att_send.at[to],
-            dst_ref=att_land.at[z],
+            dst_ref=al_land.at[z],
             send_sem=att_send_sem.at[lax.rem(to - z + nz, nz)],
             recv_sem=att_recv_sem.at[lax.rem(to - z + nz, nz)],
             device_id=(dp, to),
@@ -432,7 +530,7 @@
 
     def project(j):
         at = pl.ds(pl.multiple_of(j * rows, rows), rows)
-        normed[at, :] = layer_norm(x_land[j].astype(f32), gain, offset).astype(b16)
+        normed[at, :] = layer_norm(x_land[j].astype(f32), row(0), row(1)).astype(b16)
         for p in range(3):
             part = nt(weights_t[p * win_cols : (p + 1) * win_cols, :], normed[at, :])
             if p == 0:
@@ -518,6 +616,7 @@
 
     project(z)
     pair(z, z)
+    plane_step(early, 0)
     final = jnp.maximum(z, nz - 1 - z)
 
     def arrivals(step, carry):
@@ -533,6 +632,11 @@
         def _():
             x_start(step)
 
+        @pl.when(step == nz - 2)
+        def _():
+            for s in late:
+                s.line_start(0)
+
         high = jnp.minimum(z + step, nz)
 
         @pl.when(z - step >= 0)
@@ -543,76 +647,201 @@
         def _():
             take(z + step, jnp.maximum(z - step, 0), high, step == final)
 
-        @pl.when(step == 1)
-        def _():
-            plane_step(third, 0)
+        @pl.when(step == nz - 2)
+        def _():
             for t in range(1, steps):
-                plane_step(second, t)
-
-        @pl.when(step == 2)
-        def _():
-            for t in range(1, steps):
-                plane_step(third, t)
+                plane_step(early, t)
+            for s in early:
+                s.core_wait()
+            for s in heads:
+                s.plane_sends_wait()
+            flatten(wo_land, wo)
+            for k in range(nd * nz):
+                bias_rows[0:1, k * size_e : (k + 1) * size_e] = vec_cols[
+                    k * own : k * own + 1, 16 : 16 + size_e
+                ]
+                bias_rows[1:2, k * size_a : (k + 1) * size_a] = vec_cols[
+                    k * own + 1 : k * own + 2, 16 : 16 + size_a
+                ]
 
         return carry
 
     lax.fori_loop(1, nz, arrivals, 0)
-    own_keep = pltpu.make_async_copy(att_send.at[z], att_land.at[z], x_sem)
-    own_keep.start()
-    for s in second + third:
-        s.core_wait()
-    own_keep.wait()
+    for step in range(1, nz):
+        line_step(late, step)
+    plane_open(late)
+    for s in joints:
+        s.line_start(0)
+    al_land[z] = att_send[z]
     for off in range(1, nz):
         att_copy(lax.rem(z + off, nz)).wait()
+
+    stores = []
+
+    def store(source, to):
+        stores.append(pltpu.make_async_copy(source, to, store_sem.at[len(stores)]))
+        stores[-1].start()
+
+    step = hidden // nz
+    cols = [slice(j * step, (j + 1) * step) for j in range(nz)]
+
+    def weight(full, j):
+        return full[:, :, cols[j]].reshape(width, step)
+
+    sums[...] = jnp.zeros_like(sums)
+    sums[0:1, :] = row(0)
+    al = al_land[...].reshape(width, rows)
+    x1 = x_land[z].astype(f32) + nn(al.T, wo[...]) + row(4)
+    unit_two, inverse_two = norm_parts(x1)
+    n2 = (unit_two * row(5) + row(6)).astype(b16)
+    y = x1 + row(7)
+    plane_step(late, 0)
+    line_step(joints, 1)
+    for t in range(1, steps):
+        plane_step(late, t)
+    for j in range(nz):
+        u = nn(n2, weight(w1, j)) + bias_rows[0:1, cols[j]]
+        value, derivative = gelu_pair(u)
+        act[:, cols[j]] = value.astype(b16)
+        slope[:, cols[j]] = derivative.astype(b16)
+        if j == 1:
+            for t in range(2, nz):
+                line_step(joints, t)
+            plane_open(joints)
+    for j in range(nz):
+        y = y + nt(act[:, cols[j]], weight(w2, j))
+    block[...] = y.astype(b16)
+    store(block, block_out)
+    unit_three, inverse_three = norm_parts(y)
+    n3 = (unit_three * row(8) + row(9)).astype(b16)
+    for s in late:
+        s.core_wait()
+    flatten(wa_land, wa)
+    plane_step(joints, 0)
+    align[...] = (nn(n3, wa[...]) + bias_rows[1:2, :aligned]).astype(b16)
+    store(align, align_out)
+    ag_load.wait()
+    back = nt(ag[...], wa[...])
+    total = jnp.sum(ag[...].astype(f32), axis=0, keepdims=True)
+    at = 10 + hidden // width
+    for k in range(0, aligned, width):
+        size = min(width, aligned - k)
+        sums[at : at + 1, 0:size] = total[:, k : k + size]
+        at += 1
+    wa[...] = nn(n3.T, ag[...]).astype(b16)
+    store(wa, part_wa)
+    back, sums[8:9, :], sums[9:10, :] = norm_back(back, unit_three, inverse_three, row(8))
+    og_load.wait()
+    gy = og[...].astype(f32) + back
+    gm = gy.astype(b16)
+    sums[7:8, :] = jnp.sum(gm.astype(f32), axis=0, keepdims=True)
+    gm_t, n2_t = gm.T, n2.T
+    for s in spreads[3:5]:
+        s.line_sends_wait()
+        s.plane_sends_wait()
+    gn2 = jnp.zeros(gy.shape, f32)
+    for j in range(nz):
+        back = nn(gm, weight(w2, j))
+        w2[:, :, cols[j]] = nn(gm_t, act[:, cols[j]]).astype(b16).reshape(nd, width // nd, step)
+        store(w2.at[:, :, cols[j]], part_w2.at[:, :, cols[j]])
+        gu = (back * slope[:, cols[j]].astype(f32)).astype(b16)
+        slope[:, cols[j]] = gu
+        total = jnp.sum(gu.astype(f32), axis=0, keepdims=True)
+        for k in range(0, step, width):
+            at = (j * step + k) // width
+            sums[10 + at : 11 + at, 0:width] = total[:, k : k + width]
+        gn2 = gn2 + nt(gu, weight(w1, j))
+        if j == 1:
+            for t in range(1, steps):
+                plane_step(joints, t)
+    back, sums[5:6, :], sums[6:7, :] = norm_back(gn2, unit_two, inverse_two, row(5))
+    gx1 = gy + back
+    base[...] = gx1
+    store(base, base_out)
+    go = gx1.astype(b16)
+    sums[4:5, :] = jnp.sum(go.astype(f32), axis=0, keepdims=True)
+    grads[...] = nt(wo[...], go).astype(b16)
+    store(grads, grads_out)
+    for j in range(nz):
+        w1[:, :, cols[j]] = (
+            nn(n2_t, slope[:, cols[j]]).astype(b16).reshape(nd, width // nd, step)
+        )
+        store(w1.at[:, :, cols[j]], part_w1.at[:, :, cols[j]])
+    wo[...] = nn(al, go).astype(b16)
+    store(wo, part_wo)
+    for s in joints:
+        s.core_wait()
     for j in range(nz):
         normed_copy(j).wait()
         qkv_copy(j).wait()
         att_keep(j).wait()
-    for step in range(nz - 1):
-
-        @pl.when((z < nz - 1) & (z - step >= 0))
-        def _():
-            x_to_right(step).wait_send()
-
-        @pl.when((z > 0) & (z + step <= nz - 1))
-        def _():
-            x_to_left(step).wait_send()
-
-    for s in spreads:
-        s.sends_wait()
-
-
-def forward_call(x, vec, joint, wo, wa, w1, w2, seg_row, nd, nz, nh, cid):
+    for t in range(nz - 1):
+
+        @pl.when((z < nz - 1) & (z - t >= 0))
+        def _():
+            x_to_right(t).wait_send()
+
+        @pl.when((z > 0) & (z + t <= nz - 1))
+        def _():
+            x_to_left(t).wait_send()
+
+    for off in range(1, nz):
+        for p in range(3):
+            piece_copy(off, p).wait_send()
+    for s in spreads[:3] + spreads[5:6]:
+        s.line_sends_wait()
+    for s in spreads[:3] + spreads[5:6]:
+        s.plane_sends_wait()
+    for copy in stores:
+        copy.wait()
+
+
+def forward_call(
+    x, og, ag, vec, joint, wo, wa, w1, w2, seg_row, nd, nz, nh, size_e, size_a, cid
+):
     rows, width = x.shape
     seq, own_cols = rows * nz, nh * HD
     win_cols = -(-(own_cols + HD) // 128) * 128
     own = joint.shape[0]
+    hidden, aligned = size_e * nd * nz, ag.shape[1]
+    lines = 10 + hidden // width + -(-aligned // width)
     f32, b16 = jnp.float32, jnp.bfloat16
-    S = jax.ShapeDtypeStruct
-    na = 6
+    S, D = jax.ShapeDtypeStruct, pltpu.SemaphoreType.DMA
+    na = 7
+    wide_shape = (nd, w1.shape[0], nz * w1.shape[1])
     return pl.pallas_call(
-        functools.partial(forward_kernel, nd, nz, nh),
+        functools.partial(forward_kernel, nd, nz, nh, size_e, size_a),
         out_shape=(
-            S((16, width), f32),
+            S((rows, width), b16),
+            S((rows, aligned), b16),
+            S((rows, width), f32),
+            S((width, rows), b16),
+            S((width, width), b16),
+            S((width, aligned), b16),
+            S(wide_shape, b16),
+            S(wide_shape, b16),
+            S((lines, width), f32),
             S((nd, nz) + joint.shape, b16),
             S((nd, nz) + wo.shape, b16),
             S((nd, nz) + wa.shape, b16),
-            S((nd, w1.shape[0], nz * w1.shape[1]), b16),
-            S((nd, w2.shape[0], nz * w2.shape[1]), b16),
             S((seq, width), b16),
             S((3 * own_cols, seq), b16),
             S((own_cols, seq), f32),
             S((8, seq), f32),
-            S((nz, own_cols, rows), b16),
         ),
-        in_specs=[ANY] + [VM] * 7,
-        out_specs=(VM,) + (ANY,) * 8 + (VM, ANY),
+        in_specs=[ANY] * 3 + [VM] * 7,
+        out_specs=(ANY,) * 8 + (VM,) + (ANY,) * 6 + (VM,),
         scratch_shapes=[
+            pltpu.VMEM((nz, own_cols, rows), b16),
             pltpu.VMEM((nz, rows, width), b16),
             pltpu.VMEM((nd, nz) + vec.shape, b16),
             pltpu.VMEM((nd, nz, own, 3 * win_cols), b16),
+            pltpu.VMEM(wide_shape, b16),
+            pltpu.VMEM(wide_shape, b16),
             pltpu.VMEM((width, vec.shape[1]), f32),
-            pltpu.VMEM((width, 3 * win_cols), f32),
+            pltpu.VMEM((16, width), f32),
+            pltpu.VMEM((8, max(hidden, aligned)), f32),
+            pltpu.VMEM((width, max(width, 3 * win_cols)), f32),
             pltpu.VMEM((3 * win_cols, width), b16),
             pltpu.VMEM((3 * win_cols, rows), b16),
             pltpu.VMEM((seq, width), b16),
@@ -624,25 +853,38 @@
             pltpu.VMEM((8, seq), f32),
             pltpu.VMEM((8, seq), f32),
             pltpu.VMEM((nz, own_cols, rows), b16),
-            pltpu.SemaphoreType.DMA((na,)),
-            pltpu.SemaphoreType.DMA((na, nz)),
-            pltpu.SemaphoreType.DMA((na, nz)),
-            pltpu.SemaphoreType.DMA((na, nz)),
-            pltpu.SemaphoreType.DMA((na, 2, nd)),
-            pltpu.SemaphoreType.DMA((na, 2, nd)),
-            pltpu.SemaphoreType.DMA,
-            pltpu.SemaphoreType.DMA((nz,)),
-            pltpu.SemaphoreType.DMA((nz,)),
-            pltpu.SemaphoreType.DMA((nz,)),
-            pltpu.SemaphoreType.DMA((3,)),
-            pltpu.SemaphoreType.DMA((nz,)),
-            pltpu.SemaphoreType.DMA((nz,)),
-            pltpu.SemaphoreType.DMA((3, nz)),
+            pltpu.VMEM((rows, width), b16),
+            pltpu.VMEM((rows, aligned), b16),
+            pltpu.VMEM((width, width), b16),
+            pltpu.VMEM((width, aligned), b16),
+            pltpu.VMEM((rows, hidden), b16),
+            pltpu.VMEM((rows, hidden), b16),
+            pltpu.VMEM((rows, width), b16),
+            pltpu.VMEM((rows, aligned), b16),
+            pltpu.VMEM((rows, width), f32),
+            pltpu.VMEM((width, rows), b16),
+            D((na,)),
+            D((na, nz)),
+            D((na, nz)),
+            D((na, nz)),
+            D((na, 2, nd)),
+            D((na, 2, nd)),
+            D,
+            D((nz,)),
+            D((nz,)),
+            D((nz,)),
+            D((nz, 3)),
+            D((nz, 3)),
+            D((nz,)),
+            D((nz,)),
+            D((3, nz)),
+            D((3,)),
+            D((6 + 2 * nz,)),
         ],
         compiler_params=pltpu.CompilerParams(
-            collective_id=cid, has_side_effects=True, vmem_limit_bytes=VMEM_LIMIT
+            collective_id=cid, has_side_effects=True, vmem_limit_bytes=62 << 20
         ),
-    )(x, vec, joint, wo, wa, w1, w2, seg_row)
+    )(x, og, ag, vec, joint, wo, wa, w1, w2, seg_row)
 
 
 class Reduce:
@@ -761,12 +1003,60 @@
         for off in range(1, self.nz):
             self._line(off).wait_recv()
 
-    def line_sum(self):
-        self.line_wait()
-        total = self.chunk(self.acc, 0, self.z)[...].astype(jnp.float32)
-        for off in range(1, self.nz):
-            total = total + self.line[off].astype(jnp.float32)
-        return total
+    def _hop(self, j, way):
+        to = jnp.clip(self.z + way, 0, self.nz - 1)
+        place = j if way < 0 else jnp.where(j == to, self.nz, j)
+        return pltpu.make_async_remote_copy(
+            src_ref=self.chunk(self.acc, 0, j),
+            dst_ref=self.line.at[place],
+            send_sem=self.line_out.at[self.slot, j],
+            recv_sem=self.line_in.at[self.slot, place],
+            device_id=(self.dp, to),
+            device_id_type=MESH,
+        )
+
+    def _landed(self, place):
+        return pltpu.make_async_remote_copy(
+            src_ref=self.line.at[place],
+            dst_ref=self.line.at[place],
+            send_sem=self.line_out.at[self.slot, 0],
+            recv_sem=self.line_in.at[self.slot, place],
+            device_id=(self.dp, self.z),
+            device_id_type=MESH,
+        )
+
+    def hop(self, j, way, first):
+        @pl.when(jnp.logical_not(first))
+        def _():
+            self._landed(j).wait_recv()
+            to = self.chunk(self.acc, 0, j)
+            to[...] = (to[...].astype(jnp.float32) + self.line[j].astype(jnp.float32)).astype(to.dtype)
+
+        self._hop(j, way).start()
+
+    def home(self):
+        total = self.chunk(self.acc, 0, self.z)
+        self.total[...] = total[...].astype(jnp.float32)
+
+        @pl.when(self.z < self.nz - 1)
+        def _():
+            self._landed(self.z).wait_recv()
+            self.total[...] += self.line[self.z].astype(jnp.float32)
+
+        @pl.when(self.z > 0)
+        def _():
+            self._landed(self.nz).wait_recv()
+            self.total[...] += self.line[self.nz].astype(jnp.float32)
+
+    def hops_wait(self):
+        def step(j, carry):
+            @pl.when(j != self.z)
+            def _():
+                self._hop(j, -1).wait_send()
+
+            return carry
+
+        lax.fori_loop(0, self.nz, step, 0)
 
     def sends_wait(self):
         for m in self.masks:
@@ -775,8 +1065,6 @@
             for step in range(len(self.bits)):
                 for m, place in self.slots(half, step):
                     self._plane(half, step, m, place).wait_send()
-        for off in range(1, self.nz):
-            self._line(off).wait_send()
 
 
 def backward_kernel(
@@ -788,14 +1076,14 @@
     part_wa,
     part_w1,
     part_w2,
-    qkv,
-    att,
+    qkv_in,
+    att_in,
+    normed_in,
+    joint_in,
+    x_in,
+    base_in,
     lse,
     seg_row,
-    normed,
-    joint_full,
-    x_own,
-    base,
     vec_in,
     tokens_grad,
     out_joint,
@@ -818,6 +1106,13 @@
     vec_stage,
     vec_land,
     vec_line,
+    qkv,
+    att,
+    normed,
+    joint_full,
+    x_own,
+    base,
+    in_sem,
     *rest,
 ):
     na = 5
@@ -836,6 +1131,8 @@
         row_in,
         vec_out,
         vec_in_sem,
+        vec_line_out,
+        vec_line_in,
         own_sem,
     ) = rest[4 * na :]
     dp, z = lax.axis_index("dp"), lax.axis_index("mp")
@@ -849,9 +1146,22 @@
         Reduce(a, part, *buffers[a], wide, nd, nz, dp, z, sems) for a, (part, wide) in enumerate(parts)
     ]
     big, joint = reduces[:4], reduces[4]
+    for r, out in zip(big, (out_w2, out_w1, out_wa, out_wo)):
+        r.total = out
     steps = len(joint.bits)
 
-    greet(nd, nz, dp, z)
+    loads = [
+        pltpu.make_async_copy(source, to, in_sem.at[i])
+        for i, (source, to) in enumerate(
+            zip(
+                (qkv_in, att_in, normed_in, joint_in, x_in, base_in),
+                (qkv, att, normed, joint_full, x_own, base),
+            )
+        )
+    ]
+    for copy in loads:
+        copy.start()
+    greet(nd, nz, dp, z, everyone=True)
 
     def grad_copy(h, off):
         to = lax.rem(z + off, nz)
@@ -866,11 +1176,11 @@
 
     grad_own = pltpu.make_async_copy(grad_parts.at[z], grad_land.at[z], own_sem)
     grad_own.start()
-    for h in range(nh):
-        for off in range(1, nz):
-            grad_copy(h, off).start()
+    for off in range(1, nz):
+        grad_copy(0, off).start()
     for r in big:
         r.core_start()
+    loads[0].wait()
     for h in range(nh):
         keys[h] = qkv[own_cols + h * HD : own_cols + (h + 1) * HD, :].T
         values[h] = qkv[2 * own_cols + h * HD : 2 * own_cols + (h + 1) * HD, :].T
@@ -890,31 +1200,72 @@
         )
 
     def chores(u):
-        if u == 1:
-            big[0].core_add()
-            big[0].plane_start(0)
-        if u == 2:
+        if u == 0:
             big[1].core_add()
             big[1].plane_start(0)
-        if u == 3:
+        if u == 1:
             for r in big[2:]:
                 r.core_add()
                 r.plane_start(0)
-        if u == 5:
+        if u == 4:
             big[0].plane_add(0)
             big[0].plane_start(1)
-        if u == 8:
+        if u == 6:
+            vec_sum(1)
+        if u == 7:
             big[1].plane_add(0)
             big[1].plane_start(1)
-        if u == 10:
+        if u == 9:
             for r in big[2:]:
                 r.plane_add(0)
                 r.plane_start(1)
 
+    def vec_copy(part, off):
+        span = pl.ds(8 * part, 8)
+        return pltpu.make_async_remote_copy(
+            src_ref=vec_stage.at[0, span],
+            dst_ref=vec_land.at[off, span],
+            send_sem=vec_out.at[part, off],
+            recv_sem=vec_in_sem.at[part, off],
+            device_id=(lax.rem(dp + off, nd), z),
+            device_id_type=MESH,
+        )
+
+    def vec_line_copy(part, off):
+        span = pl.ds(8 * part, 8)
+        return pltpu.make_async_remote_copy(
+            src_ref=vec_stage.at[1, span],
+            dst_ref=vec_line.at[off, span],
+            send_sem=vec_line_out.at[part, off],
+            recv_sem=vec_line_in.at[part, off],
+            device_id=(dp, lax.rem(z + off, nz)),
+            device_id_type=MESH,
+        )
+
+    def vec_sum(part):
+        span = slice(8 * part, 8 * part + 8)
+        total = vec_stage[0, span, :]
+        for off in range(1, nd):
+            vec_copy(part, off).wait_recv()
+            total = total + vec_land[off, span, :]
+        vec_stage[1, span, :] = total
+        for off in range(1, nz):
+            vec_line_copy(part, off).start()
+
+    vec_stage[0] = vec_in[...]
+    for off in range(1, nd):
+        vec_copy(1, off).start()
+    big[0].core_add()
+    big[0].plane_start(0)
     grad_own.wait()
+    loads[1].wait()
     for h in range(nh):
         for off in range(1, nz):
             grad_copy(h, off).wait_recv()
+        if h == 0:
+            for later in range(1, nh):
+                for off in range(1, nz):
+                    grad_copy(later, off).start()
         key_grad[...] = jnp.zeros_like(key_grad)
         value_grad[...] = jnp.zeros_like(value_grad)
 
@@ -972,6 +1323,35 @@
                 )
             bias_cols[at, col : col + 1] = total
 
+    def stream(r, way):
+        def left(j, carry):
+            r.hop(j, -1, z == nz - 1)
+            return carry
+
+        def right(k, carry):
+            r.hop(nz - 1 - k, 1, z == 0)
+            return carry
+
+        if way < 0:
+            lax.fori_loop(0, z, left, 0)
+        else:
+            lax.fori_loop(0, nz - 1 - z, right, 0)
+
+    for r in big:
+        for t in range(1, steps):
+            r.plane_add(t)
+            r.plane_start(t + 1)
+
+        @pl.when(z == nz - 1)
+        def _():
+            stream(r, -1)
+
+        @pl.when(z == 0)
+        def _():
+            stream(r, 1)
+
+    for copy in loads[2:]:
+        copy.wait()
     grad_t = jnp.zeros((3 * own_cols, width), f32)
     for j in range(nz):
         grad_t = grad_t + nn(
@@ -984,18 +1364,22 @@
             at = (d * nz + j) * own
             part_joint[d, j] = grad_joint[at : at + own, :].astype(b16)
     joint.core_start()
-    for t in range(1, steps):
-        for r in big:
-            r.plane_add(t)
-            r.plane_start(t + 1)
-    for r in big:
-        r.line_start()
     joint.core_add()
     joint.plane_start(0)
     for t in range(steps):
         joint.plane_add(t)
         joint.plane_start(t + 1)
     joint.line_start()
+
+    @pl.when((z > 0) & (z < nz // 2))
+    def _():
+        for r in big:
+            stream(r, 1)
+
+    @pl.when((z >= nz // 2) & (z < nz - 1))
+    def _():
+        for r in big:
+            stream(r, -1)
 
     for h in range(nh):
         for off in range(1, nz):
@@ -1014,62 +1398,58 @@
         - unit * jnp.mean(scaled * unit, axis=-1, keepdims=True)
     )
     bias_rows = bias_cols[...].T
-    vec_stage[0] = vec_in[...]
     vec_stage[0, 0:1, :] = jnp.sum(back * unit, axis=0, keepdims=True)
     vec_stage[0, 1:2, :] = jnp.sum(back, axis=0, keepdims=True)
     vec_stage[0, 2:4, :] = bias_rows[0:2, :]
-    bits = [1] + joint.bits
-
-    def vec_copy(t):
-        return pltpu.make_async_remote_copy(
-            src_ref=vec_stage.at[t],
-            dst_ref=vec_land.at[t],
-            send_sem=vec_out.at[t],
-            recv_sem=vec_in_sem.at[t],
-            device_id=(peer_flip(dp, bits[t]), z),
-            device_id_type=MESH,
-        )
-
-    def vec_line_copy(off):
-        return pltpu.make_async_remote_copy(
-            src_ref=vec_stage.at[len(bits)],
-            dst_ref=vec_line.at[off],
-            send_sem=vec_out.at[len(bits) + off],
-            recv_sem=vec_in_sem.at[len(bits) + off],
-            device_id=(dp, lax.rem(z + off, nz)),
-            device_id_type=MESH,
-        )
-
-    for t in range(len(bits)):
-        vec_copy(t).start()
-        vec_copy(t).wait_recv()
-        vec_stage[t + 1] = vec_stage[t] + vec_land[t]
+    for off in range(1, nd):
+        vec_copy(0, off).start()
+
+    @pl.when((z > 0) & (z < nz // 2))
+    def _():
+        for r in big:
+            stream(r, -1)
+
+    @pl.when((z >= nz // 2) & (z < nz - 1))
+    def _():
+        for r in big:
+            stream(r, 1)
+
+    vec_sum(0)
+
+    for r in big:
+        r.home()
+    joint.line_wait()
+    joint.line[0] = joint.acc[0, z]
+    for j in range(nz):
+        piece = joint.line[lax.rem(z - j + nz, nz)].astype(f32)
+        for p in range(3):
+            out_joint[:, p * width + j * own_cols : p * width + (j + 1) * own_cols] = piece[
+                :, p * own_cols : (p + 1) * own_cols
+            ]
+    total = vec_stage[1]
     for off in range(1, nz):
-        vec_line_copy(off).start()
-    for r, out in zip(big, (out_w2, out_w1, out_wa, out_wo)):
-        out[...] = r.line_sum()
-    joint.line_wait()
-    out_joint[z] = joint.acc[0, z].astype(f32)
-    for off in range(1, nz):
-        out_joint[lax.rem(z - off + nz, nz)] = joint.line[off].astype(f32)
-    total = vec_stage[len(bits)]
-    for off in range(1, nz):
-        vec_line_copy(off).wait_recv()
+        for part in range(2):
+            vec_line_copy(part, off).wait_recv()
         total = total + vec_line[off]
     out_vec[...] = total
-    for t in range(len(bits)):
-        vec_copy(t).wait_send()
+    for part in range(2):
+        for off in range(1, nd):
+            vec_copy(part, off).wait_send()
+        for off in range(1, nz):
+            vec_line_copy(part, off).wait_send()
     for off in range(1, nz):
-        vec_line_copy(off).wait_send()
         for h in range(nh):
             grad_copy(h, off).wait_send()
             row_copy(h, off).wait_send()
+        joint._line(off).wait_send()
     for r in reduces:
         r.sends_wait()
+    for r in big:
+        r.hops_wait()
 
 
 def backward_call(
-    grad_parts, wo, wa, w1, w2, qkv, att, lse, seg_row, normed, joint_full, x_own, base, vec_in, nd, nz, nh, cid
+    grad_parts, wo, wa, w1, w2, qkv, att, normed, joint_full, x_own, base, lse, seg_row, vec_in, nd, nz, nh, cid
 ):
     rows, width = x_own.shape
     seq, own_cols = rows * nz, nh * HD
@@ -1080,26 +1460,26 @@
     held = []
     for shape, wide in ((w2.shape, True), (w1.shape, True), (wa.shape, False), (wo.shape, False), (joint_shape, False)):
         piece = shape[1:]
-        line = (nz, piece[0], piece[1] // nz) if wide else piece
+        line = (nz + 1, piece[0], piece[1] // nz) if wide else (nz + 1,) + piece[1:]
         held += [
             pltpu.VMEM((nd // 2,) + piece, b16),
             pltpu.VMEM((nd // 2,) + piece, b16),
             pltpu.VMEM((max(nd // 2 - 1, 1),) + piece, b16),
             pltpu.VMEM(line, b16),
         ]
-    na, nb = 5, nd.bit_length() - 1
+    na = 5
     return pl.pallas_call(
         functools.partial(backward_kernel, nd, nz, nh),
         out_shape=(
             S((rows, width), f32),
-            S((nz, own, 3 * own_cols), f32),
+            S((own, 3 * width), f32),
             S(wo.shape[2:], f32),
             S(wa.shape[2:], f32),
             S((w1.shape[1], w1.shape[2] // nz), f32),
             S((w2.shape[1], w2.shape[2] // nz), f32),
             S(vec_in.shape, f32),
         ),
-        in_specs=[ANY] * 5 + [VM] * 9,
+        in_specs=[ANY] * 11 + [VM] * 3,
         out_specs=(VM,) * 7,
         scratch_shapes=[
             pltpu.VMEM((nz, own_cols, rows), b16),
@@ -1113,9 +1493,16 @@
             pltpu.VMEM(joint_shape, b16),
             pltpu.VMEM((width, 128), f32),
             pltpu.VMEM((seq, 128), jnp.int32),
-            pltpu.VMEM((nb + 1,) + vec_in.shape, f32),
-            pltpu.VMEM((nb,) + vec_in.shape, f32),
+            pltpu.VMEM((2,) + vec_in.shape, f32),
+            pltpu.VMEM((nd,) + vec_in.shape, f32),
             pltpu.VMEM((nz,) + vec_in.shape, f32),
+            pltpu.VMEM(qkv.shape, b16),
+            pltpu.VMEM(att.shape, f32),
+            pltpu.VMEM(normed.shape, b16),
+            pltpu.VMEM(joint_full.shape, b16),
+            pltpu.VMEM(x_own.shape, b16),
+            pltpu.VMEM(base.shape, f32),
+            D((6,)),
         ]
         + held
         + [
@@ -1124,236 +1511,22 @@
             D((na, nd // 2)),
             D((na, 2, nd // 2)),
             D((na, 2, nd // 2)),
-            D((na, nz)),
-            D((na, nz)),
+            D((na, nz + 1)),
+            D((na, nz + 1)),
             D((nh, nz)),
             D((nh, nz)),
             D((nh, nz)),
             D((nh, nz)),
-            D((nb + nz,)),
-            D((nb + nz,)),
+            D((2, nd)),
+            D((2, nd)),
+            D((2, nz)),
+            D((2, nz)),
             D,
         ],
         compiler_params=pltpu.CompilerParams(
-            collective_id=cid, has_side_effects=True, vmem_limit_bytes=60 << 20
+            collective_id=cid, has_side_effects=True, vmem_limit_bytes=63 << 20
         ),
-    )(grad_parts, wo, wa, w1, w2, qkv, att, lse, seg_row, normed, joint_full, x_own, base, vec_in)
-
-
-def gelu_pair(u):
-    size = jnp.abs(u)
-    t = 1.0 / (1.0 + (0.3275911 * 0.7071067811865476) * size)
-    poly = ((((1.061405429 * t - 1.453152027) * t + 1.421413741) * t - 0.284496736) * t + 0.254829592) * t
-    bell = jnp.exp(-0.5 * u * u)
-    tail = 0.5 * poly * bell
-    share = jnp.where(u >= 0.0, 1.0 - tail, tail)
-    return u * share, share + u * (0.3989422804014327 * bell)
-
-
-def norm_parts(values):
-    centre = values - jnp.mean(values, axis=-1, keepdims=True)
-    inverse = lax.rsqrt(jnp.mean(centre * centre, axis=-1, keepdims=True) + EPSILON)
-    return centre * inverse, inverse
-
-
-def norm_back(grad, unit, inverse, gain):
-    scaled = grad * gain
-    back = inverse * (
-        scaled
-        - jnp.mean(scaled, axis=-1, keepdims=True)
-        - unit * jnp.mean(scaled * unit, axis=-1, keepdims=True)
-    )
-    return (
-        back,
-        jnp.sum(grad * unit, axis=0, keepdims=True),
-        jnp.sum(grad, axis=0, keepdims=True),
-    )
-
-
-def middle_kernel(
-    pieces,
-    nz,
-    al_in,
-    x_in,
-    og_in,
-    ag_in,
-    wo_in,
-    wa_in,
-    w1_in,
-    w2_in,
-    vec,
-    expand_bias,
-    align_bias,
-    block_out,
-    align_out,
-    base,
-    grad_parts,
-    part_wo,
-    part_wa,
-    part_w1,
-    part_w2,
-    sums,
-    al,
-    x,
-    og,
-    ag,
-    wo,
-    wa,
-    w1,
-    w2,
-    act,
-    slope,
-    block,
-    align,
-    base_v,
-    grads,
-    own_wo,
-    own_wa,
-    own_w1,
-    own_w2,
-    load_sem,
-    store_sem,
-):
-    f32, b16 = jnp.float32, jnp.bfloat16
-    width = x.shape[1]
-    hidden = w1.shape[1]
-    step = hidden // pieces
-    cols = [slice(j * step, (j + 1) * step) for j in range(pieces)]
-    loads = {}
-
-    def load(name, source, to):
-        loads[name] = pltpu.make_async_copy(source, to, load_sem.at[len(loads)])
-        loads[name].start()
-
-    load("wo", wo_in, wo)
-    load("al", al_in, al)
-    load("x", x_in, x)
-    for j in range(pieces):
-        load(("w1", j), w1_in.at[:, cols[j]], w1.at[:, cols[j]])
-        load(("w2", j), w2_in.at[:, cols[j]], w2.at[:, cols[j]])
-    load("wa", wa_in, wa)
-    load("ag", ag_in, ag)
-    load("og", og_in, og)
-    stores = []
-
-    def store(source, to):
-        stores.append(pltpu.make_async_copy(source, to, store_sem.at[len(stores)]))
-        stores[-1].start()
-
-    def row(i):
-        return vec[i : i + 1, :]
-
-    sums[...] = jnp.zeros_like(sums)
-    sums[0:1, :] = row(0)
-    for name in ("wo", "al", "x"):
-        loads[name].wait()
-    x1 = x[...].astype(f32) + nn(al[...].T, wo[...]) + row(4)
-    unit_two, inverse_two = norm_parts(x1)
-    n2 = (unit_two * row(5) + row(6)).astype(b16)
-    y = x1 + row(7)
-    for j in range(pieces):
-        loads["w1", j].wait()
-        u = nn(n2, w1[:, cols[j]]) + expand_bias[:, cols[j]]
-        value, derivative = gelu_pair(u)
-        act[:, cols[j]] = value.astype(b16)
-        slope[:, cols[j]] = derivative.astype(b16)
-    for j in range(pieces):
-        loads["w2", j].wait()
-        y = y + nt(act[:, cols[j]], w2[:, cols[j]])
-    block[...] = y.astype(b16)
-    store(block, block_out)
-    unit_three, inverse_three = norm_parts(y)
-    n3 = (unit_three * row(8) + row(9)).astype(b16)
-    loads["wa"].wait()
-    loads["ag"].wait()
-    align[...] = (nn(n3, wa[...]) + align_bias[...]).astype(b16)
-    store(align, align_out)
-    own_wa[...] = nn(n3.T, ag[...]).astype(b16)
-    store(own_wa, part_wa)
-    aligned = jnp.sum(ag[...].astype(f32), axis=0, keepdims=True)
-    done = 0
-    at = 10 + hidden // width
-    while done < aligned.shape[1]:
-        size = min(width, aligned.shape[1] - done)
-        sums[at : at + 1, 0:size] = aligned[:, done : done + size]
-        done, at = done + size, at + 1
-    back, sums[8:9, :], sums[9:10, :] = norm_back(
-        nt(ag[...], wa[...]), unit_three, inverse_three, row(8)
-    )
-    loads["og"].wait()
-    gy = og[...].astype(f32) + back
-    gm = gy.astype(b16)
-    sums[7:8, :] = jnp.sum(gm.astype(f32), axis=0, keepdims=True)
-    gm_t, n2_t = gm.T, n2.T
-    gn2 = jnp.zeros(gy.shape, f32)
-    for j in range(pieces):
-        own_w2[:, cols[j]] = nn(gm_t, act[:, cols[j]]).astype(b16)
-        store(own_w2.at[:, cols[j]], part_w2.at[:, cols[j]])
-        gu = (nn(gm, w2[:, cols[j]]) * slope[:, cols[j]].astype(f32)).astype(b16)
-        slope[:, cols[j]] = gu
-        total = jnp.sum(gu.astype(f32), axis=0, keepdims=True)
-        for k in range(0, step, width):
-            at = (j * step + k) // width
-            sums[10 + at : 11 + at, (j * step + k) % width : (j * step + k) % width + min(step, width)] = (
-                total[:, k : k + width]
-            )
-        gn2 = gn2 + nt(gu, w1[:, cols[j]])
-    back, sums[5:6, :], sums[6:7, :] = norm_back(gn2, unit_two, inverse_two, row(5))
-    gx1 = gy + back
-    base_v[...] = gx1
-    store(base_v, base)
-    go = gx1.astype(b16)
-    sums[4:5, :] = jnp.sum(go.astype(f32), axis=0, keepdims=True)
-    grads[...] = nt(wo[...], go).astype(b16)
-    store(grads, grad_parts)
-    for j in range(pieces):
-        own_w1[:, cols[j]] = nn(n2_t, slope[:, cols[j]]).astype(b16)
-        store(own_w1.at[:, cols[j]], part_w1.at[:, cols[j]])
-    own_wo[...] = nn(al[...], go).astype(b16)
-    store(own_wo, part_wo)
-    for s in stores:
-        s.wait()
-
-
-def middle_call(al, x, og, ag, wo, wa, w1, w2, vec, expand_bias, align_bias, nz):
-    f32, b16 = jnp.float32, jnp.bfloat16
-    S = jax.ShapeDtypeStruct
-    rows, width = x.shape
-    hidden, wide = w1.shape[1], wa.shape[1]
-    pieces = 4
-    shapes = [al, x, og, ag, wo, wa, w1, w2]
-    return pl.pallas_call(
-        functools.partial(middle_kernel, pieces, nz),
-        out_shape=(
-            S((rows, width), b16),
-            S((rows, wide), b16),
-            S((rows, width), f32),
-            S((width, rows), b16),
-            S(wo.shape, b16),
-            S(wa.shape, b16),
-            S(w1.shape, b16),
-            S(w2.shape, b16),
-            S(vec.shape, f32),
-        ),
-        in_specs=[ANY] * 8 + [VM] * 3,
-        out_specs=(ANY,) * 8 + (VM,),
-        scratch_shapes=[pltpu.VMEM(a.shape, b16) for a in shapes]
-        + [
-            pltpu.VMEM((rows, hidden), b16),
-            pltpu.VMEM((rows, hidden), b16),
-            pltpu.VMEM((rows, width), b16),
-            pltpu.VMEM((rows, wide), b16),
-            pltpu.VMEM((rows, width), f32),
-            pltpu.VMEM((width, rows), b16),
-            pltpu.VMEM(wo.shape, b16),
-            pltpu.VMEM(wa.shape, b16),
-            pltpu.VMEM(w1.shape, b16),
-            pltpu.VMEM(w2.shape, b16),
-            pltpu.SemaphoreType.DMA((6 + 2 * pieces,)),
-            pltpu.SemaphoreType.DMA((6 + 2 * pieces,)),
-        ],
-        compiler_params=pltpu.CompilerParams(vmem_limit_bytes=60 << 20),
-    )(al, x, og, ag, wo, wa, w1, w2, vec, expand_bias, align_bias)
+    )(grad_parts, wo, wa, w1, w2, qkv, att, normed, joint_full, x_own, base, lse, seg_row, vec_in)
 
 
 def local(
@@ -1401,17 +1574,38 @@
         reduce_bias,
         head_gain,
         head_shift,
-        expand_bias,
-        align_bias,
     )
-    flat, at = 0.0, 0
-    for v in small:
-        flat = flat + jnp.pad(v, (at, 16 * own - at - v.shape[0]))
-        at += v.shape[0]
-    vec = jnp.pad(flat.reshape(16, own).T, ((0, 0), (0, 112)))
+    flat = 0.0
+    for i, v in enumerate(small):
+        flat = flat + jnp.pad(v, (i * own, (15 - i) * own))
+    size_e, size_a = expand_bias.shape[0], align_bias.shape[0]
+    vec = (
+        jnp.pad(flat.reshape(16, own).T, ((0, 0), (0, 112)))
+        + jnp.pad(expand_bias[None], ((0, own - 1), (16, 112 - size_e)))
+        + jnp.pad(align_bias[None], ((1, own - 2), (16, 112 - size_a)))
+    )
     seg_row = segments.reshape(1, seq)
-    vectors, joint_full, wo, wa, w1, w2, normed_all, qkv, att, lse, attended = forward_call(
+    (
+        block_out,
+        align_out,
+        base,
+        grad_parts,
+        p_wo,
+        p_wa,
+        p_w1,
+        p_w2,
+        vec_in,
+        joint_full,
+        _,
+        _,
+        normed_all,
+        qkv,
+        att,
+        lse,
+    ) = forward_call(
         tokens,
+        out_grad,
+        align_grad,
         vec,
         joint_weight,
         output_weight,
@@ -1422,68 +1616,35 @@
         nd,
         nz,
         nh,
+        size_e,
+        size_a,
         1,
     )
     joint_full = joint_full.reshape(width, 3 * width)
-    output_full = wo.reshape(width, width)
-    align_full = wa.reshape(width, -1)
-    expand_full = w1.reshape(width, -1)
-    reduce_full = w2.reshape(width, -1)
-    attended = attended.reshape(width, rows)
-    count = -(-expand_bias.shape[0] // own)
-    bias_expand = (
-        vectors[10 : 10 + count].reshape(count, n, own).transpose(1, 0, 2).reshape(n, count * own)
-    )[:, : expand_bias.shape[0]].reshape(-1)
-    count_align = -(-align_bias.shape[0] // own)
-    bias_align = (
-        vectors[10 + count : 10 + count + count_align]
-        .reshape(count_align, n, own)
-        .transpose(1, 0, 2)
-        .reshape(n, count_align * own)
-    )[:, : align_bias.shape[0]].reshape(-1)
-
-    block_out, align_out, base, grad_parts, p_wo, p_wa, p_w1, p_w2, vec_in = middle_call(
-        attended,
-        tokens,
-        out_grad,
-        align_grad,
-        output_full,
-        align_full,
-        expand_full,
-        reduce_full,
-        vectors,
-        bias_expand[None],
-        bias_align[None],
-        nz,
-    )
-    hidden = expand_full.shape[1]
-    tokens_grad, joint_mine, g_wo, g_wa, g_w1, g_w2, sums = backward_call(
+    hidden = size_e * n
+    tokens_grad, g_joint, g_wo, g_wa, g_w1, g_w2, sums = backward_call(
         grad_parts.reshape(nz, own_cols, rows),
         p_wo.reshape(nd, nz, own, width),
         p_wa.reshape(nd, nz, own, -1),
-        p_w1.reshape(nd, width // nd, hidden),
-        p_w2.reshape(nd, width // nd, hidden),
+        p_w1,
+        p_w2,
         qkv,
         att,
-        lse,
-        seg_row,
         normed_all,
         joint_full,
         tokens,
         base,
+        lse,
+        seg_row,
         vec_in,
         nd,
         nz,
         nh,
         2,
     )
-    g_joint = (
-        joint_mine.reshape(nz, own, 3, own_cols).transpose(1, 2, 0, 3).reshape(own, 3 * width)
-    )
     me = lax.axis_index("dp") * nz + z
     mine = lax.dynamic_slice_in_dim(sums[:10], me * own, own, axis=1)
     flat = sums[10:].reshape(-1)
-    size_e, size_a = expand_bias.shape[0], align_bias.shape[0]
     g_expand_b = lax.dynamic_slice_in_dim(flat, me * size_e, size_e)
     g_align_b = lax.dynamic_slice_in_dim(flat, hidden + me * size_a, size_a)
     return (

time: 292 us -> 276 us (0.945)
  Pallas kernels: 274 us -> 259 us
    pallas_call x1, Pallas kernels: 119 us -> 107 us  [backward_call(): pl.pallas_call(functools.partial(backward_kernel, nd, nz, nh), out_shape=...]
    pallas_call x2 -> x1, Pallas kernels: 155 us -> 152 us  [forward_call(): pl.pallas_call(functools.partial(forward_kernel, nd, nz, nh, size_e, size...]
    unnamed x17 -> x24, local copies, waits for them, and re-layouts: 3.87 us -> 6.42 us
where the time goes in v1:
time: 276 us; the launch traced here: 272 us
  Pallas kernels  259 us (94%)
  local copies, waits for them, and re-layouts  10.2 us (4%)
    pallas_call x1, Pallas kernels, forward_call(): pl.pallas_call(functools.partial(forward_kernel, nd, nz, nh, size_e, size...  152 us
    pallas_call x1, Pallas kernels, backward_call(): pl.pallas_call(functools.partial(backward_kernel, nd, nz, nh), out_shape=...  107 us
    unnamed x24, local copies, waits for them, and re-layouts  6.42 us

profile of v1, /device:TPU:0, one launch (start us, length us, event | category | flops | bytes accessed | tf_op | source)
XLA Modules:
  0.0 272.2 jit_solution(11401683439418362730)
XLA Ops:
  0.7 0.9 pad_add_fusion.1
  1.5 0.1 reshape.58
  1.6 0.1 copy.41
  1.7 1.4 pad_add_fusion.vec_own
  3.1 151.8 %shard_map.356 = (bf16[512,768]{1,0:T(8,128)(2,1)}, bf16[512,1024]{1,0:T(8,128)(2,1)}, f32[512,768]{1,0:T(8,128)}, bf16[768,512]{1,0:T(8,128)(2,1)}, bf16[768,76...) custom-call(bf16[512,768]{1,0:T(8,128)(2,1)} %x_in.1, ...), custom_call_target="tpu_custom_call" | custom-call | tf_op jit(solution)/shard_map/pallas_call | solution.py:812
  154.8 0.0 copy-start.2
  154.8 106.8 %shard_map.357 = (f32[512,768]{1,0:T(8,128)}, f32[24,2304]{1,0:T(8,128)}, f32[24,768]{1,0:T(8,128)}, f32[24,1024]{1,0:T(8,128)}, f32[96,768]{1,0:T(8,128)}, /*index=5*/f32[96,768]{1,0:T(8,128)}, f32[16,768]{1,0:T(8,128)}) custom-call(bf16[4,192,512]{2,1,0:T(8,128)(2,1)} %bitcast.33, bf16[8,4,24,768]{3,2,1,0:T(8,128)(2,1)} %bitcast.32, ...), custom_call_target="tpu_custom_call" | custom-call | tf_op jit(solution)/shard_map/pallas_call | solution.py:1471
  261.7 0.0 copy-start.1
  261.7 0.8 slice.44
  262.5 0.6 dynamic_slice.11
  263.1 0.6 dynamic_slice.10
  263.7 1.6 dynamic-slice_bitcast_fusion
  265.3 0.0 copy-done.2
  265.3 0.0 copy-start
  265.3 0.9 copy.50
  266.2 1.0 copy.51
  267.2 1.1 copy.52
  268.4 0.0 copy-done.5
  268.4 0.7 copy.53
  269.1 0.0 copy-done.7
  269.1 0.6 copy.54
  269.7 0.6 copy.55
  270.3 0.7 copy.56
  271.1 0.7 copy.57
  (11 shorter events, 0.0 us)
Async XLA Ops:
  154.8 110.5 %copy-start.2 = (bf16[512,768]{1,0:T(8,128)(2,1)S(1)}, bf16[512,768]{1,0:T(8,128)(2,1)}, u32[]{:S(2)}) copy-start(bf16[512,768]{1,0:T(8,128)(2,1)} %get-tuple-element.92) | copy-start | bytes 2359300
  261.7 4.5 %copy-start.1 = (bf16[512,1024]{1,0:T(8,128)(2,1)S(1)}, bf16[512,1024]{1,0:T(8,128)(2,1)}, u32[]{:S(2)}) copy-start(bf16[512,1024]{1,0:T(8,128)(2,1)} %get-tuple-element.93) | copy-start | bytes 3145732
  265.3 1.9 copy-start
  267.2 1.2 copy-start.5
  267.2 1.9 copy-start.7
  267.2 2.5 copy-start.6
  267.2 3.1 %copy-start.4 = (f32[96,768]{1,0:T(8,128)S(1)}, f32[96,768]{1,0:T(8,128)}, u32[]{:S(2)}) copy-start(f32[96,768]{1,0:T(8,128)} %get-tuple-element.110) | copy-start | bytes 884740
  267.2 3.8 %copy-start.3 = (f32[96,768]{1,0:T(8,128)S(1)}, f32[96,768]{1,0:T(8,128)}, u32[]{:S(2)}) copy-start(f32[96,768]{1,0:T(8,128)} %get-tuple-element.61) | copy-start | bytes 884740

commit v2 on v1

--- a/solution.py
+++ b/solution.py
@@ -491,20 +491,32 @@
     bias_q = vec_cols[pl.ds(win, win_cols), 2:3]
     bias_v = vec_cols[pl.ds(win, win_cols), 3:4]
 
-    def flatten(source, to):
-        cols = to.shape[1]
-        part = cols // -(-cols // window.shape[-1])
-        for k in range(0, cols, part):
-            load = pltpu.make_async_copy(
-                source.at[:, :, :, pl.ds(k, part)], window.at[:, :, :, pl.ds(0, part)], load_sem.at[2]
-            )
-            load.start()
-            load.wait()
+    slots = 3
+    part = window.shape[-1] // slots
+
+    def flatten_load(source, k):
+        return pltpu.make_async_copy(
+            source.at[:, :, :, pl.ds(k * part, part)],
+            window.at[:, :, :, pl.ds(k % slots * part, part)],
+            load_sem.at[2 + k % slots],
+        )
+
+    def flatten_start(source, to):
+        for k in range(min(slots, to.shape[1] // part)):
+            flatten_load(source, k).start()
+
+    def flatten_finish(source, to):
+        count = to.shape[1] // part
+        for k in range(count):
+            flatten_load(source, k).wait()
+            lanes = slice(k % slots * part, (k % slots + 1) * part)
             for d in range(nd):
                 for j in range(nz):
                     at = (d * nz + j) * own
-                    weights[at : at + own, :part] = window[d, j, :, :part].astype(f32)
-            to[:, k : k + part] = weights[:, :part].astype(b16)
+                    weights[at : at + own, lanes] = window[d, j, :, lanes].astype(f32)
+            to[:, k * part : (k + 1) * part] = weights[:, lanes].astype(b16)
+            if k + slots < count:
+                flatten_load(source, k + slots).start()
 
     def normed_copy(j):
         at = pl.ds(pl.multiple_of(j * rows, rows), rows)
@@ -617,6 +629,15 @@
     project(z)
     pair(z, z)
     plane_step(early, 0)
+    for k in range(nd * nz):
+        bias_rows[0:1, k * size_e : (k + 1) * size_e] = vec_cols[
+            k * own : k * own + 1, 16 : 16 + size_e
+        ]
+        bias_rows[1:2, k * size_a : (k + 1) * size_a] = vec_cols[
+            k * own + 1 : k * own + 2, 16 : 16 + size_a
+        ]
+    for s in heads:
+        s.plane_sends_wait()
     final = jnp.maximum(z, nz - 1 - z)
 
     def arrivals(step, carry):
@@ -637,6 +658,11 @@
             for s in late:
                 s.line_start(0)
 
+        @pl.when(step == nz - 1)
+        def _():
+            for t in range(1, steps):
+                plane_step(early[:2], t)
+
         high = jnp.minimum(z + step, nz)
 
         @pl.when(z - step >= 0)
@@ -646,23 +672,6 @@
         @pl.when(z + step <= nz - 1)
         def _():
             take(z + step, jnp.maximum(z - step, 0), high, step == final)
-
-        @pl.when(step == nz - 2)
-        def _():
-            for t in range(1, steps):
-                plane_step(early, t)
-            for s in early:
-                s.core_wait()
-            for s in heads:
-                s.plane_sends_wait()
-            flatten(wo_land, wo)
-            for k in range(nd * nz):
-                bias_rows[0:1, k * size_e : (k + 1) * size_e] = vec_cols[
-                    k * own : k * own + 1, 16 : 16 + size_e
-                ]
-                bias_rows[1:2, k * size_a : (k + 1) * size_a] = vec_cols[
-                    k * own + 1 : k * own + 2, 16 : 16 + size_a
-                ]
 
         return carry
 
@@ -672,6 +681,11 @@
     plane_open(late)
     for s in joints:
         s.line_start(0)
+    early[0].core_wait()
+    flatten_start(wo_land, wo)
+    for t in range(1, steps):
+        plane_step(early[2:], t)
+    flatten_finish(wo_land, wo)
     al_land[z] = att_send[z]
     for off in range(1, nz):
         att_copy(lax.rem(z + off, nz)).wait()
@@ -699,6 +713,7 @@
     line_step(joints, 1)
     for t in range(1, steps):
         plane_step(late, t)
+    early[1].core_wait()
     for j in range(nz):
         u = nn(n2, weight(w1, j)) + bias_rows[0:1, cols[j]]
         value, derivative = gelu_pair(u)
@@ -708,15 +723,17 @@
             for t in range(2, nz):
                 line_step(joints, t)
             plane_open(joints)
+    for s in late:
+        s.core_wait()
+    flatten_start(wa_land, wa)
+    early[2].core_wait()
     for j in range(nz):
         y = y + nt(act[:, cols[j]], weight(w2, j))
     block[...] = y.astype(b16)
     store(block, block_out)
     unit_three, inverse_three = norm_parts(y)
     n3 = (unit_three * row(8) + row(9)).astype(b16)
-    for s in late:
-        s.core_wait()
-    flatten(wa_land, wa)
+    flatten_finish(wa_land, wa)
     plane_step(joints, 0)
     align[...] = (nn(n3, wa[...]) + bias_rows[1:2, :aligned]).astype(b16)
     store(align, align_out)
@@ -878,7 +895,7 @@
             D((nz,)),
             D((nz,)),
             D((3, nz)),
-            D((3,)),
+            D((5,)),
             D((6 + 2 * nz,)),
         ],
         compiler_params=pltpu.CompilerParams(
@@ -1529,6 +1546,40 @@
     )(grad_parts, wo, wa, w1, w2, qkv, att, normed, joint_full, x_own, base, lse, seg_row, vec_in)
 
 
+def finish_kernel(n, own, size_e, size_a, sums, *refs):
+    count = (len(refs) - 12) // 2
+    for source, to in zip(refs[:count], refs[count : 2 * count]):
+        to[...] = source[...]
+    mine = refs[-12:]
+    me = lax.axis_index("dp") * lax.axis_size("mp") + lax.axis_index("mp")
+    width = sums.shape[1]
+    hidden = size_e * n
+    for k in range(n):
+
+        @pl.when(me == k)
+        def _():
+            for i in range(10):
+                mine[i][...] = sums[i : i + 1, k * own : (k + 1) * own]
+            at = k * size_e
+            line = 10 + at // width
+            mine[10][...] = sums[line : line + 1, at % width : at % width + size_e]
+            at = k * size_a
+            line = 10 + hidden // width + at // width
+            mine[11][...] = sums[line : line + 1, at % width : at % width + size_a]
+
+
+def finish_call(sums, results, n, own, size_e, size_a):
+    S = jax.ShapeDtypeStruct
+    return pl.pallas_call(
+        functools.partial(finish_kernel, n, own, size_e, size_a),
+        out_shape=tuple(S(r.shape, r.dtype) for r in results)
+        + tuple(S((1, size), jnp.float32) for size in (own,) * 10 + (size_e, size_a)),
+        in_specs=[VM] * (1 + len(results)),
+        out_specs=(VM,) * (len(results) + 12),
+        compiler_params=pltpu.CompilerParams(vmem_limit_bytes=VMEM_LIMIT),
+    )(sums, *results)
+
+
 def local(
     tokens,
     segments,
@@ -1642,11 +1693,15 @@
         nh,
         2,
     )
-    me = lax.axis_index("dp") * nz + z
-    mine = lax.dynamic_slice_in_dim(sums[:10], me * own, own, axis=1)
-    flat = sums[10:].reshape(-1)
-    g_expand_b = lax.dynamic_slice_in_dim(flat, me * size_e, size_e)
-    g_align_b = lax.dynamic_slice_in_dim(flat, hidden + me * size_a, size_a)
+    block_out, align_out, tokens_grad, g_joint, g_wo, g_wa, g_w1, g_w2, *mine = finish_call(
+        sums,
+        (block_out, align_out, tokens_grad, g_joint, g_wo, g_wa, g_w1, g_w2),
+        n,
+        own,
+        size_e,
+        size_a,
+    )
+    mine = [v.reshape(-1) for v in mine]
     return (
         block_out,
         align_out,
@@ -1660,12 +1715,12 @@
         mine[4],
         mine[5],
         mine[6],
-        g_expand_b,
+        mine[10],
         mine[7],
         mine[8],
         mine[9],
         g_wa,
-        g_align_b,
+        mine[11],
         g_w1,
         g_w2.T,
     )

time: 276 us -> 270 us (0.978)
  local copies, waits for them, and re-layouts: 10.2 us -> 0.17 us
  Pallas kernels: 259 us -> 263 us
    unnamed x24 -> x0, local copies, waits for them, and re-layouts: 6.42 us -> none
    pallas_call x0 -> x1, Pallas kernels: none -> 4.78 us  [finish_call(): pl.pallas_call(functools.partial(finish_kernel, n, own, size_e, size_a),...]
where the time goes in v2:
time: 270 us; the launch traced here: 267 us
  Pallas kernels  263 us (97%)
    pallas_call x1, Pallas kernels, forward_call(): pl.pallas_call(functools.partial(forward_kernel, nd, nz, nh, size_e, size...  152 us
    pallas_call x1, Pallas kernels, backward_call(): pl.pallas_call(functools.partial(backward_kernel, nd, nz, nh), out_shape=...  107 us

profile of v2, /device:TPU:0, one launch (start us, length us, event | category | flops | bytes accessed | tf_op | source)
XLA Modules:
  0.0 266.7 jit_solution(7357252110686783985)
XLA Ops:
  0.7 0.9 pad_add_fusion.1
  1.5 0.1 reshape.91
  1.6 0.1 copy.41
  1.7 1.4 pad_add_fusion.vec_own
  3.1 151.7 %shard_map.356 = (bf16[512,768]{1,0:T(8,128)(2,1)}, bf16[512,1024]{1,0:T(8,128)(2,1)}, f32[512,768]{1,0:T(8,128)}, bf16[768,512]{1,0:T(8,128)(2,1)}, bf16[768,76...) custom-call(bf16[512,768]{1,0:T(8,128)(2,1)} %x_in.1, ...), custom_call_target="tpu_custom_call" | custom-call | tf_op jit(solution)/shard_map/pallas_call | solution.py:829
  154.7 106.7 %shard_map.357 = (f32[512,768]{1,0:T(8,128)}, f32[24,2304]{1,0:T(8,128)}, f32[24,768]{1,0:T(8,128)}, f32[24,1024]{1,0:T(8,128)}, f32[96,768]{1,0:T(8,128)}, /*index=5*/f32[96,768]{1,0:T(8,128)}, f32[16,768]{1,0:T(8,128)}) custom-call(bf16[4,192,512]{2,1,0:T(8,128)(2,1)} %bitcast.24, bf16[8,4,24,768]{3,2,1,0:T(8,128)(2,1)} %bitcast.23, ...), custom_call_target="tpu_custom_call" | custom-call | tf_op jit(solution)/shard_map/pallas_call | solution.py:1488
  261.5 4.8 %shard_map.358 = (bf16[512,768]{1,0:T(8,128)(2,1)}, bf16[512,1024]{1,0:T(8,128)(2,1)}, f32[512,768]{1,0:T(8,128)}, f32[24,2304]{1,0:T(8,128)}, f32[24,768]{1,0:T...) custom-call(f32[16,768]{1,0:T(8,128)} %get-tuple-element.73.sums, ...), custom_call_target="tpu_custom_call" | custom-call | tf_op jit(solution)/shard_map/pallas_call | solution.py:1573
